TPU v7x, 512 devices: a whole 4x4x16 slice. The times are simulated.
512 devices in a mesh: group: 8 (over x, core), dev: 64 (over z, y).
Axes of the slice: x: 4, y: 4, z: 16, core: 2. Of those that a mesh axis runs over, the one named last changes fastest.
Arguments:
- cam_jac: float32 [2, 9, 8, 262144], P(None, None, None, ('group', 'dev')), may hold values from -6 to 6
- lm_jac: float32 [2, 3, 8, 262144], P(None, None, None, ('group', 'dev')), may hold values from -6 to 6
- resid: float32 [2, 8, 262144], P(None, None, ('group', 'dev')), may hold values from -6 to 6
- cam_index: int32 [8, 262144], P(None, ('group', 'dev')), may hold values from 0 to 8191
Outputs:
- camera_step: float32 [9, 8192], P(None, 'dev')
- camera_residual: float32 [9, 8192], P(None, 'dev')
- landmark_step: float32 [3, 262144], P(None, ('group', 'dev'))
Inputs may be any that keep to these rules, and one draw needn't show every extreme that they name: `cam_index`: every observation names one of the 8192 cameras.
All inputs are finite; a program needn't handle non-finite values.
Results may differ from a plain program's by a relative error of at most 0.0003.
Values sent between devices are 32-bit elements; how exact they have to be, the bound alone decides.
A program may use at most 64 MiB of HBM per device.

v0:
```python
import jax
import jax.numpy as jnp
from jax import lax
from jax.sharding import PartitionSpec as P

CAM_DEV = 128
ITERS = 2


DAMPING = 1.0


def landmark_inverse(lm_jac):

    def entry(first, second):
        return jnp.sum(lm_jac[:, first] * lm_jac[:, second], axis=(0, 1))

    w_00 = entry(0, 0) + DAMPING
    w_11 = entry(1, 1) + DAMPING
    w_22 = entry(2, 2) + DAMPING
    w_01 = entry(0, 1)
    w_02 = entry(0, 2)
    w_12 = entry(1, 2)
    cof_00 = w_11 * w_22 - w_12 * w_12
    cof_01 = w_02 * w_12 - w_01 * w_22
    cof_02 = w_01 * w_12 - w_02 * w_11
    cof_11 = w_00 * w_22 - w_02 * w_02
    cof_12 = w_01 * w_02 - w_00 * w_12
    cof_22 = w_00 * w_11 - w_01 * w_01
    determinant = w_00 * cof_00 + w_01 * cof_01 + w_02 * cof_02
    rows = [
        jnp.stack([cof_00, cof_01, cof_02]),
        jnp.stack([cof_01, cof_11, cof_12]),
        jnp.stack([cof_02, cof_12, cof_22]),
    ]
    return jnp.stack(rows) / determinant[None, None]


def apply_inverse(inverse, vector):
    return jnp.sum(inverse * vector[None], axis=1)


def landmark_side(lm_jac, values):
    return jnp.sum(lm_jac * values[:, None], axis=(0, 2))


def back_project(lm_jac, landmark):
    return jnp.sum(lm_jac * landmark[None, :, None, :], axis=1)


def camera_apply(cam_jac, cam_values):
    return jnp.sum(cam_jac * cam_values[None], axis=1)


def camera_transpose(cam_jac, errors):
    return jnp.sum(cam_jac * errors[:, None], axis=0)


def to_cameras(values, cam_index, total_cams):
    flat_index = cam_index.reshape(-1)
    width = values.shape[0]

    def one_row(column):
        return jax.ops.segment_sum(column, flat_index, num_segments=total_cams)

    return jax.vmap(one_row)(values.reshape(width, -1))


def schur_obs(cam_jac, lm_jac, inverse, cam_values):
    applied = camera_apply(cam_jac, cam_values)
    landmark = apply_inverse(inverse, landmark_side(lm_jac, applied))
    return camera_transpose(cam_jac, applied - back_project(lm_jac, landmark))


def gather_cameras(tile):
    return lax.all_gather(tile, "dev", axis=1, tiled=True)


def reduce_cameras(terms):
    totals = lax.psum(terms, ("group", "dev"))
    width = terms.shape[1] // lax.axis_size("dev")
    return lax.dynamic_slice_in_dim(totals, lax.axis_index("dev") * width, width, 1)


def inner_product(left, right):
    return lax.psum(jnp.sum(left * right), "dev")


def body(cam_jac, lm_jac, resid, cam_index):
    total_cams = CAM_DEV * lax.axis_size("dev")
    inverse = landmark_inverse(lm_jac)
    land_rhs = apply_inverse(inverse, landmark_side(lm_jac, resid))
    errors = resid - back_project(lm_jac, land_rhs)
    stacked = jnp.concatenate(
        [camera_transpose(cam_jac, errors), jnp.sum(cam_jac * cam_jac, axis=0)], axis=0
    )
    summed = reduce_cameras(to_cameras(stacked, cam_index, total_cams))
    gradient = summed[:9]
    diagonal = summed[9:] + DAMPING
    residual = gradient
    precond = residual / diagonal
    direction = precond
    rz_now = inner_product(residual, precond)
    solution = jnp.zeros_like(gradient)
    for iteration in range(ITERS):
        whole = gather_cameras(direction)
        cam_values = jnp.take(whole, cam_index, axis=1)
        terms = to_cameras(schur_obs(cam_jac, lm_jac, inverse, cam_values), cam_index, total_cams)
        image = reduce_cameras(terms) + DAMPING * direction
        alpha = rz_now / inner_product(direction, image)
        solution = solution + alpha * direction
        residual = residual - alpha * image
        if iteration + 1 < ITERS:
            precond = residual / diagonal
            rz_next = inner_product(residual, precond)
            direction = precond + rz_next / rz_now * direction
            rz_now = rz_next
    whole_step = gather_cameras(solution)
    cam_obs = camera_apply(cam_jac, jnp.take(whole_step, cam_index, axis=1))
    landmark_step = land_rhs - apply_inverse(inverse, landmark_side(lm_jac, cam_obs))
    return (solution, residual, landmark_step)


def solution(mesh):
    in_specs = (
        P(None, None, None, ("group", "dev")),
        P(None, None, None, ("group", "dev")),
        P(None, None, ("group", "dev")),
        P(None, ("group", "dev")),
    )
    out_specs = (P(None, "dev"), P(None, "dev"), P(None, ("group", "dev")))
    return jax.shard_map(body, mesh=mesh, in_specs=in_specs, out_specs=out_specs, check_vma=False)
```

profile of v0, /device:TPU:8, one launch (start us, length us, event | category | flops | bytes accessed | tf_op | source)
XLA Modules:
  0.0 2390.0 jit_solution(14837299796872105308)
XLA Ops:
  7.2 0.0 all-reduce.5.cloned.1.call-start
  7.2 0.8 multiply_reduce_fusion.22
  8.0 0.9 multiply_reduce_fusion.13
  9.0 0.7 copy.31
  9.8 0.9 multiply_reduce_fusion.12
  10.7 0.8 sub.128
  11.5 1.0 multiply_reduce_fusion.6
  12.5 0.6 copy.28
  13.2 0.0 copy-start.2
  13.2 24.5 %scatter_custom_fusion = f32[18,8192]{0,1:T(8,128)} fusion(s32[4096]{0:T(1024)S(1)} %bitcast.43, f32[4096,18]{1,0:T(8,128)S(1)} %bitcast.38, f32[]{:T(128)} %constant.14.clone.1), kind=kCustom, calls=%fused_computation.13 | custom fusion | flops 73728 | bytes 589828 | tf_op jit(solution)/shard_map/vmap()/scatter-add | solution.py:64
  37.7 0.0 all-reduce.5.cloned.1.call-update
  37.8 0.0 all-reduce.7.cloned.1.call-start
  37.8 0.0 copy-done.2
  37.9 494.2 %all-reduce.5.cloned.1.call-done = f32[18,8192]{0,1:T(8,128)} async-done(((f32[18,8192]{0,1:T(8,128)}), f32[18,8192]{0,1:T(8,128)}) %all-reduce.5.cloned.1.call-update) | async-done | bytes 589840 | tf_op jit(solution)/shard_map/psum | solution.py:80
  532.1 1.0 fusion.7
  533.1 111.9 %all_gather.9 = f32[9,8192]{0,1:T(8,128)} all-gather(f32[9,128]{0,1:T(8,128)S(1)} %fusion.7), channel_id=1, replica_groups=mesh['group'=8,'dev'=64] {'dev'}, dimensions={1}, use_global_device_ids=true | all-gather | bytes 299520 | tf_op jit(solution)/shard_map/all_gather | solution.py:76
  645.0 0.0 copy-start
  645.0 0.0 copy-start.1
  645.0 16.3 gather_fusion
  661.3 1.9 select_bitcast_fusion.2
  663.3 0.6 copy.21
  663.9 0.0 copy-done
  664.0 0.0 copy-done.1
  664.1 0.6 copy.29
  664.8 24.5 %scatter_custom_fusion.1 = f32[9,8192]{0,1:T(8,128)} fusion(s32[4096]{0:T(1024)S(1)} %bitcast.44, f32[4096,9]{1,0:T(8,128)S(1)} %bitcast.40, f32[]{:T(128)} %constant.14.clone.1), kind=kCustom, calls=%fused_computation.11 | custom fusion | flops 36864 | bytes 294916 | tf_op jit(solution)/shard_map/vmap()/scatter-add | solution.py:64
  689.3 0.0 all-reduce.7.cloned.1.call-update
  689.3 0.0 all-reduce.9.cloned.1.call-start
  689.4 488.0 %all-reduce.7.cloned.1.call-done = f32[9,8192]{0,1:T(8,128)} async-done(((f32[9,8192]{0,1:T(8,128)}), f32[9,8192]{0,1:T(8,128)}) %all-reduce.7.cloned.1.call-update) | async-done | bytes 294928 | tf_op jit(solution)/shard_map/psum | solution.py:80
  1177.4 1.6 multiply_reduce_fusion.16
  1179.0 139.5 %all-reduce = (f32[]{:T(128)}, f32[]{:T(128)}) all-reduce(f32[]{:T(128)} %get-tuple-element.22, f32[]{:T(128)} %get-tuple-element.21), channel_id=1, replica_groups=mesh['group'=8,'dev'=64] {'dev'}, use_global_device_ids=true, to_apply=%region_14.0 | all-reduce | flops 2 | bytes 16 | tf_op jit(solution)/shard_map/psum | solution.py:86
  1319.8 1.6 multiply_reduce_fusion.15
  1321.4 140.7 %psum.53 = f32[]{:T(128)} all-reduce(f32[]{:T(128)} %get-tuple-element.25), channel_id=1, replica_groups=mesh['group'=8,'dev'=64] {'dev'}, use_global_device_ids=true, to_apply=%region_25.27 | all-reduce | flops 1 | bytes 8 | tf_op jit(solution)/shard_map/psum | solution.py:86
  1463.5 1.0 multiply_add_fusion.1
  1464.5 110.5 %all_gather.10 = f32[9,8192]{0,1:T(8,128)} all-gather(f32[9,128]{0,1:T(8,128)S(1)} %multiply_add_fusion.1), channel_id=1, replica_groups=mesh['group'=8,'dev'=64] {'dev'}, dimensions={1}, use_global_device_ids=true | all-gather | bytes 299520 | tf_op jit(solution)/shard_map/all_gather | solution.py:76
  1575.0 16.3 gather_fusion.1
  1591.2 1.9 select_bitcast_fusion.1
  1593.2 0.6 copy.23
  1594.0 0.6 copy.30
  1594.6 24.5 %scatter_custom_fusion.2 = f32[9,8192]{0,1:T(8,128)} fusion(s32[4096]{0:T(1024)S(1)} %bitcast.45, f32[4096,9]{1,0:T(8,128)S(1)} %bitcast.39, f32[]{:T(128)} %constant.14.clone.1), kind=kCustom, calls=%fused_computation.9 | custom fusion | flops 36864 | bytes 294916 | tf_op jit(solution)/shard_map/vmap()/scatter-add | solution.py:64
  1619.2 0.0 all-reduce.9.cloned.1.call-update
  1619.2 488.2 %all-reduce.9.cloned.1.call-done = f32[9,8192]{0,1:T(8,128)} async-done(((f32[9,8192]{0,1:T(8,128)}), f32[9,8192]{0,1:T(8,128)}) %all-reduce.9.cloned.1.call-update) | async-done | bytes 294928 | tf_op jit(solution)/shard_map/psum | solution.py:80
  2107.4 1.5 multiply_reduce_fusion.14
  2108.9 139.4 %psum.55 = f32[]{:T(128)} all-reduce(f32[]{:T(128)} %multiply_reduce_fusion.14), channel_id=1, replica_groups=mesh['group'=8,'dev'=64] {'dev'}, use_global_device_ids=true, to_apply=%region_34.36 | all-reduce | flops 1 | bytes 8 | tf_op jit(solution)/shard_map/psum | solution.py:86
  2249.7 1.0 multiply_subtract_fusion
  2250.7 0.7 copy.26
  2251.4 111.8 %all_gather.11 = f32[9,8192]{0,1:T(8,128)} all-gather(f32[9,128]{0,1:T(8,128)S(1)} %get-tuple-element.34), channel_id=1, replica_groups=mesh['group'=8,'dev'=64] {'dev'}, dimensions={1}, use_global_device_ids=true | all-gather | bytes 299520 | tf_op jit(solution)/shard_map/all_gather | solution.py:76
  2363.2 0.7 copy.27
  2363.9 16.3 gather_fusion.2
  2380.2 1.9 select_bitcast_fusion
  2382.1 0.6 copy.25
  2382.8 0.6 sub.133
  (23 shorter events, 0.5 us)
Async XLA Ops:
  7.2 524.9 %all-reduce.5.cloned.1.call-start = ((), (), s32[]{:S(2)}) async-start(), calls=%async_computation | async-start | bytes 8388608 | tf_op jit(solution)/shard_map/psum | solution.py:80
  13.2 24.6 %copy-start.2 = (s32[8,512]{1,0:T(8,128)S(1)}, s32[8,512]{1,0:T(8,128)}, u32[]{:S(2)}) copy-start(s32[8,512]{1,0:T(8,128)} %param.9) | copy-start | bytes 49156
  37.8 1139.6 %all-reduce.7.cloned.1.call-start = ((), (), s32[]{:S(2)}) async-start(), calls=%async_computation.1 | async-start | bytes 8388608 | tf_op jit(solution)/shard_map/psum | solution.py:80
  645.0 18.9 copy-start
  645.0 19.0 copy-start.1
  689.3 1418.1 %all-reduce.9.cloned.1.call-start = ((), (), s32[]{:S(2)}) async-start(), calls=%async_computation.2 | async-start | bytes 8388608 | tf_op jit(solution)/shard_map/psum | solution.py:80
Sparse Core Ops, SparseCore 0:
  37.9 494.1 all-reduce.4
  689.4 487.8 all-reduce.6
  1619.3 488.0 all-reduce.8
where the time goes:
time: 2390 us
  waiting for transfers between devices  1470 us (62%)
  blocking collectives  754 us (32%)
  other arithmetic  92.8 us (4%)
  local copies, waits for them, and re-layouts  54.8 us (2%)
    psum x3, waiting for transfers between devices, reduce_cameras(): totals = lax.psum(terms, ('group', 'dev'))  1470 us
    psum x3, blocking collectives, inner_product(): return lax.psum(jnp.sum(left * right), 'dev')  420 us
    all_gather x3, blocking collectives, gather_cameras(): return lax.all_gather(tile, 'dev', axis=1, tiled=True)  334 us
    scatter-add x3, other arithmetic, one_row(): return jax.ops.segment_sum(column, flat_index, num_segments=total_cams)  73.6 us
  transfers between devices with their start and end apart: 3, of which 3 were waited for; matrix products, arithmetic and copies ran while one was open for 0% of the time, Pallas kernels for 0%

commit v1 on v0

v1 whole, which is shorter than its diff:
```python
import functools

import jax
import jax.numpy as jnp
from jax import lax
from jax.experimental import pallas as pl
from jax.experimental.pallas import tpu as pltpu
from jax.sharding import PartitionSpec as P

DAMPING = 1.0
MESH = pl.DeviceIdType.MESH
F32 = jnp.float32
BF16 = jnp.bfloat16

TILE = 24
K = 8
LM = 512
OBS = K * LM


def split(value):
    high = value.astype(BF16).astype(F32)
    return high, value - high


def rows_sum(value):
    return jnp.sum(value, axis=0, keepdims=True)


def kernel(cj, lj, rs, ci, step_o, res_o, lm_o,
           onehot, tag8, tag16, hot_q, lhs_a, lhs_b, fld_a, fld_b, nat, err, inv, q_sc,
           terms1, terms2, terms3, core1, core2, core3, xy1, xy2, xy3,
           zl1, zl2, zl3, zh1, zh2, zh3, field1, field2, field3, fin,
           s_core, r_core, s_xy, r_xy, s_zl, r_zl, s_zh, r_zh, s_gx, r_gx, s_gc, r_gc, s_fin, r_fin):
    group = lax.axis_index("group")
    dev = lax.axis_index("dev")
    x, c = group // 2, group % 2
    z, y = dev // 4, dev % 4
    xy = x * 4 + y
    zl, zh = z % 4, z // 4

    def at(xx, cc, yy, zz):
        return {"group": xx * 2 + cc, "dev": zz * 4 + yy}

    sibling = at(x, 1 - c, y, z)
    plane = []
    for k in (10, 6, 14, 9, 11, 2, 8, 5, 7, 13, 15, 1, 3, 4, 12):
        xx, yy = (x + k // 4) % 4, (y + k % 4) % 4
        plane.append((xx * 4 + yy, at(xx, c, yy, z)))
    z_low = [((zl + k) % 4, at(x, c, y, zh * 4 + (zl + k) % 4)) for k in (2, 1, 3)]
    z_high = [((zh + k) % 4, at(x, c, y, ((zh + k) % 4) * 4 + zl)) for k in (2, 1, 3)]
    final = []
    for k in (2, 1, 3, 0):
        for o in (1, 0):
            if k or o:
                xx, cc = (x + k) % 4, (c + o) % 2
                final.append((xx * 2 + cc, at(xx, cc, y, z)))

    barrier = pltpu.get_barrier_semaphore()
    others = [sibling] + [d for _, d in plane + z_low + z_high]
    others += [d for (s, d), (k, o) in zip(final, [(k, o) for k in (2, 1, 3, 0) for o in (1, 0) if k or o]) if k and o]
    for d in others:
        pl.semaphore_signal(barrier, inc=1, device_id=d, device_id_type=MESH)

    iota256 = lax.broadcasted_iota(jnp.int32, (256, LM), 0)
    iota32 = lax.broadcasted_iota(jnp.int32, (32, LM), 0)
    for k in range(K):
        ks = pl.ds(k * LM, LM)
        cam = ci[k:k + 1, :]
        low = (cam >> 9) * 16 + (cam & 15)
        tag = ((cam >> 4) & 1) * 16 + ((cam >> 5) & 3) * 4 + ((cam >> 7) & 3)
        onehot[:, ks] = jnp.where(iota256 == low, 1.0, 0.0).astype(BF16)
        hot_q[:, ks] = jnp.where(iota32 == tag, 1.0, 0.0).astype(BF16)
        tag8[:, ks] = jnp.broadcast_to(tag, (8, LM))
        tag16[:, ks] = jnp.broadcast_to(tag.astype(F32), (16, LM)).astype(BF16)

    def put_terms(base_a, base_b, k, first8, last):
        ks = pl.ds(k * LM, LM)
        both = jnp.concatenate(split(first8), axis=0).astype(BF16)
        tags = tag16[:, ks]
        for q in range(32):
            lhs_a[base_a + q * 16:base_a + q * 16 + 16, ks] = jnp.where(tags == BF16(q), both, BF16(0))
        high, low = split(last)
        hot = hot_q[:, ks]
        lhs_b[base_b:base_b + 32, ks] = hot * jnp.broadcast_to(high, (32, LM)).astype(BF16)
        lhs_b[base_b + 32:base_b + 64, ks] = hot * jnp.broadcast_to(low, (32, LM)).astype(BF16)

    def dot_t(left, right):
        return lax.dot_general(left, right, (((1,), (1,)), ((), ())), preferred_element_type=F32)

    iota_rows = lax.broadcasted_iota(jnp.int32, (8, 128), 0)

    def scatter(terms, base_a, base_b, row, scalar):
        out_a = dot_t(lhs_a[base_a:base_a + 512, :], onehot[...])
        out_b = dot_t(lhs_b[base_b:base_b + 64, :], onehot[...])
        last = out_b[0:32] + out_b[32:64]
        for q in range(32):
            both = out_a[q * 16:q * 16 + 8] + out_a[q * 16 + 8:q * 16 + 16]
            terms[q // 16, q % 16, row:row + 8, :] = both[:, 0:128]
            terms[q // 16, q % 16, row + 8:row + 16, :] = both[:, 128:256]
            terms[q // 16, q % 16, row + 16:row + 24, :] = jnp.where(
                iota_rows == 0, last[q:q + 1, 0:128], jnp.where(
                    iota_rows == 1, last[q:q + 1, 128:256], jnp.where(iota_rows == 2, scalar, 0.0)))

    def push(src, dst, send, recv, device):
        copy = pltpu.make_async_remote_copy(
            src_ref=src, dst_ref=dst, send_sem=send, recv_sem=recv, device_id=device, device_id_type=MESH)
        copy.start()
        return copy

    def landed(dst, sem):
        pltpu.make_async_copy(dst, dst, sem).wait()

    def total(buf, count):
        out = buf[0]
        for k in range(1, count):
            out = out + buf[k]
        return out

    def exchange(n, source, own, mine, partners, buf, s_sem, r_sem, copies):
        for i, (slot, device) in enumerate(partners):
            copies.append(push(source(slot), buf.at[mine], s_sem.at[n, i], r_sem.at[n, mine], device))
        if own is not None:
            buf[mine] = own
        for slot, _ in partners:
            landed(buf.at[slot], r_sem.at[n, slot])

    def reduce(n, terms, core_buf, xy_buf, zl_buf, zh_buf, copies):
        copy = push(terms.at[1 - c], core_buf, s_core.at[n], r_core.at[n], sibling)
        copies.append(copy)
        landed(core_buf, r_core.at[n])
        terms[c] = terms[c] + core_buf[...]
        exchange(n, lambda s: terms.at[c, s], terms[c, xy], xy, plane, xy_buf, s_xy, r_xy, copies)
        zl_buf[zl] = total(xy_buf, 16)
        exchange(n, lambda s: zl_buf.at[zl], None, zl, z_low, zl_buf, s_zl, r_zl, copies)
        zh_buf[zh] = total(zl_buf, 4)
        exchange(n, lambda s: zh_buf.at[zh], None, zh, z_high, zh_buf, s_zh, r_zh, copies)
        return total(zh_buf, 4)

    def gather(n, tile, field, copies):
        field[c, xy] = tile
        for i, (slot, device) in enumerate(plane):
            copies.append(push(field.at[c, xy], field.at[c, xy], s_gx.at[n, i], r_gx.at[n, xy], device))
        for slot, _ in plane:
            landed(field.at[c, slot], r_gx.at[n, slot])
        copies.append(push(field.at[c], field.at[c], s_gc.at[n], r_gc.at[n], sibling))
        landed(field.at[1 - c], r_gc.at[n])

    def entry(first, second):
        return rows_sum(lj[0, first] * lj[0, second] + lj[1, first] * lj[1, second])

    w_00 = entry(0, 0) + DAMPING
    w_11 = entry(1, 1) + DAMPING
    w_22 = entry(2, 2) + DAMPING
    w_01 = entry(0, 1)
    w_02 = entry(0, 2)
    w_12 = entry(1, 2)
    cof_00 = w_11 * w_22 - w_12 * w_12
    cof_01 = w_02 * w_12 - w_01 * w_22
    cof_02 = w_01 * w_12 - w_02 * w_11
    cof_11 = w_00 * w_22 - w_02 * w_02
    cof_12 = w_01 * w_02 - w_00 * w_12
    cof_22 = w_00 * w_11 - w_01 * w_01
    determinant = w_00 * cof_00 + w_01 * cof_01 + w_02 * cof_02
    for i, cof in enumerate((cof_00, cof_01, cof_02, cof_11, cof_12, cof_22)):
        inv[i:i + 1, :] = cof / determinant

    def eliminate(a0, a1, where):
        side = [rows_sum(lj[0, j] * a0 + lj[1, j] * a1) for j in range(3)]
        picks = ((0, 1, 2), (1, 3, 4), (2, 4, 5))
        e0, e1 = a0, a1
        for j in range(3):
            q = sum(inv[p:p + 1, :] * side[m] for m, p in enumerate(picks[j]))
            q_sc[where * 3 + j:where * 3 + j + 1, :] = q
            e0 = e0 - lj[0, j] * q
            e1 = e1 - lj[1, j] * q
        err[0] = e0
        err[1] = e1
        return e0, e1

    def cam_rows(i, k):
        return cj[i, 0:8, k, :]

    copies = []

    e0, e1 = eliminate(rs[0], rs[1], 0)
    grad_last = cj[0, 8] * e0 + cj[1, 8] * e1
    diag_last = cj[0, 8] * cj[0, 8] + cj[1, 8] * cj[1, 8]
    nat[0] = grad_last
    nat[1] = diag_last
    for k in range(K):
        c0, c1 = cam_rows(0, k), cam_rows(1, k)
        put_terms(0, 0, k, c0 * err[0, k:k + 1, :] + c1 * err[1, k:k + 1, :], nat[0, k:k + 1, :])
        put_terms(512, 64, k, c0 * c0 + c1 * c1, nat[1, k:k + 1, :])
    zero = jnp.zeros((1, 128), F32)
    scatter(terms1, 0, 0, 0, zero)
    scatter(terms1, 512, 64, TILE, zero)

    pl.semaphore_wait(barrier, len(others))

    summed = reduce(0, terms1, core1, xy1, zl1, zh1, copies)
    iota_tile = lax.broadcasted_iota(jnp.int32, (TILE, 128), 0)
    real = iota_tile < 18

    def inner(left, right):
        return jnp.sum(jnp.where(real, left * right, 0.0), keepdims=True)

    residual = jnp.where(real, summed[0:TILE], 0.0)
    diagonal = jnp.where(real, summed[TILE:2 * TILE], 0.0) + DAMPING
    precond = residual / diagonal
    gather(0, jnp.where(iota_tile == 18, inner(residual, precond), precond), field1, copies)

    def rz_total(field):
        out = field[0, 0, 18:19, :]
        for q in range(1, 32):
            out = out + field[q // 16, q % 16, 18:19, :]
        return out

    def load_field(field):
        square = jnp.zeros((8, 128), F32)
        for q in range(32):
            part = field[q // 16, q % 16]
            h0, l0 = split(part[0:8])
            h1, l1 = split(part[8:16])
            fld_a[q * 16:q * 16 + 16, 0:128] = jnp.concatenate([h0, l0], axis=0).astype(BF16)
            fld_a[q * 16:q * 16 + 16, 128:256] = jnp.concatenate([h1, l1], axis=0).astype(BF16)
            square = square + part[0:8] * part[0:8] + part[8:16] * part[8:16]
        for half in range(2):
            last = jnp.concatenate([field[0, :, 16 + half, :], field[1, :, 16 + half, :]], axis=0)
            high, low = split(last)
            fld_b[0:32, half * 128:half * 128 + 128] = high.astype(BF16)
            fld_b[32:64, half * 128:half * 128 + 128] = low.astype(BF16)
            for s in range(4):
                square = square + last[s * 8:s * 8 + 8] * last[s * 8:s * 8 + 8]
        return jnp.sum(square, keepdims=True)

    def apply(field, where, terms):
        square = load_field(field)
        for k in range(K):
            ks = pl.ds(k * LM, LM)
            out_a = jnp.dot(fld_a[...], onehot[:, ks], preferred_element_type=F32)
            out_b = jnp.dot(fld_b[...], onehot[:, ks], preferred_element_type=F32)
            tags = tag8[:, ks]
            high, low = out_a[0:8], out_a[8:16]
            for q in range(1, 32):
                hit = tags == q
                high = jnp.where(hit, out_a[q * 16:q * 16 + 8], high)
                low = jnp.where(hit, out_a[q * 16 + 8:q * 16 + 16], low)
            values = high + low
            last = rows_sum((out_b[0:32] + out_b[32:64]) * hot_q[:, ks].astype(F32))
            for i in range(2):
                nat[i, k:k + 1, :] = rows_sum(cam_rows(i, k) * values)
            nat[2, k:k + 1, :] = last
        a0 = nat[0] + cj[0, 8] * nat[2]
        a1 = nat[1] + cj[1, 8] * nat[2]
        e0, e1 = eliminate(a0, a1, where)
        nat[0] = cj[0, 8] * e0 + cj[1, 8] * e1
        product = jnp.sum(a0 * e0 + a1 * e1, keepdims=True)
        for k in range(K):
            put_terms(0, 0, k, cam_rows(0, k) * err[0, k:k + 1, :] + cam_rows(1, k) * err[1, k:k + 1, :], nat[0, k:k + 1, :])
        scatter(terms, 0, 0, 0, jnp.broadcast_to(product, (1, 128)))
        return square

    rz = rz_total(field1)
    square = apply(field1, 1, terms2)
    image = reduce(1, terms2, core2, xy2, zl2, zh2, copies)
    direction = jnp.where(real, field1[c, xy], 0.0)
    alpha1 = rz / (image[18:19] + DAMPING * square)
    residual = residual - alpha1 * jnp.where(real, image + DAMPING * direction, 0.0)
    precond = residual / diagonal
    gather(1, jnp.where(iota_tile == 18, inner(residual, precond), precond), field2, copies)

    rz_next = rz_total(field2)
    beta = rz_next / rz
    for h in range(2):
        for q in range(16):
            field3[h, q] = field2[h, q] + beta * field1[h, q]
    square = apply(field3, 2, terms3)
    image = reduce(2, terms3, core3, xy3, zl3, zh3, copies)
    direction2 = jnp.where(real, field3[c, xy], 0.0)
    alpha2 = rz_next / (image[18:19] + DAMPING * square)
    residual = residual - alpha2 * jnp.where(real, image + DAMPING * direction2, 0.0)
    step = alpha1 * direction + alpha2 * direction2

    low_half = z < 8
    pieces = jnp.concatenate([
        jnp.where(low_half, step[0:8], step[8:16]),
        jnp.where(low_half, residual[0:8], residual[8:16]),
        jnp.where(iota_rows == 0, jnp.where(low_half, step[16:17], step[17:18]),
                  jnp.where(iota_rows == 1, jnp.where(low_half, residual[16:17], residual[17:18]), 0.0)),
    ], axis=0)
    moved = pltpu.roll(pieces, (group * 16 - (z % 8) * 16 + 128) % 128, 1)
    lane = lax.broadcasted_iota(jnp.int32, (TILE, 128), 1)
    fin[group] = jnp.where(lane // 16 == group, moved, 0.0)
    for i, (slot, device) in enumerate(final):
        copies.append(push(fin.at[group], fin.at[group], s_fin.at[i], r_fin.at[group], device))

    scale1 = jnp.concatenate([alpha1] * 4, axis=1)
    scale2 = jnp.concatenate([alpha2] * 4, axis=1)
    lm_o[...] = q_sc[0:3, :] - scale1 * q_sc[3:6, :] - scale2 * q_sc[6:9, :]

    for slot, _ in final:
        landed(fin.at[slot], r_fin.at[slot])
    whole = total(fin, 8)
    step_o[0:8, :] = whole[0:8]
    step_o[8:9, :] = whole[16:17]
    res_o[0:8, :] = whole[8:16]
    res_o[8:9, :] = whole[17:18]
    for copy in copies:
        copy.wait_send()


def body(cam_jac, lm_jac, resid, cam_index):
    vmem = pl.BlockSpec(memory_space=pltpu.VMEM)

    def tiles(*lead):
        return pltpu.VMEM(lead + (TILE, 128), F32)

    def wide(*lead):
        return pltpu.VMEM(lead + (2 * TILE, 128), F32)

    dma = pltpu.SemaphoreType.DMA
    scratch = [
        pltpu.VMEM((256, OBS), BF16), pltpu.VMEM((8, OBS), jnp.int32), pltpu.VMEM((16, OBS), BF16), pltpu.VMEM((32, OBS), BF16),
        pltpu.VMEM((1024, OBS), BF16), pltpu.VMEM((128, OBS), BF16), pltpu.VMEM((512, 256), BF16), pltpu.VMEM((64, 256), BF16),
        pltpu.VMEM((3, K, LM), F32), pltpu.VMEM((2, K, LM), F32), pltpu.VMEM((8, LM), F32), pltpu.VMEM((16, LM), F32),
        wide(2, 16), tiles(2, 16), tiles(2, 16), wide(16), tiles(16), tiles(16), wide(16), tiles(16), tiles(16),
        wide(4), tiles(4), tiles(4), wide(4), tiles(4), tiles(4), tiles(2, 16), tiles(2, 16), tiles(2, 16), tiles(8),
        dma((3,)), dma((3,)), dma((3, 15)), dma((3, 16)), dma((3, 3)), dma((3, 4)), dma((3, 3)), dma((3, 4)),
        dma((2, 15)), dma((2, 16)), dma((2,)), dma((2,)), dma((7,)), dma((8,)),
    ]
    return pl.pallas_call(
        kernel,
        out_shape=(jax.ShapeDtypeStruct((9, 128), F32), jax.ShapeDtypeStruct((9, 128), F32), jax.ShapeDtypeStruct((3, LM), F32)),
        in_specs=[vmem] * 4,
        out_specs=(vmem, vmem, vmem),
        scratch_shapes=scratch,
        name="schur_cg",
        compiler_params=pltpu.CompilerParams(collective_id=0, has_side_effects=True, vmem_limit_bytes=56 << 20),
    )(cam_jac, lm_jac, resid, cam_index)


def solution(mesh):
    in_specs = (
        P(None, None, None, ("group", "dev")),
        P(None, None, None, ("group", "dev")),
        P(None, None, ("group", "dev")),
        P(None, ("group", "dev")),
    )
    out_specs = (P(None, "dev"), P(None, "dev"), P(None, ("group", "dev")))
    return jax.shard_map(body, mesh=mesh, in_specs=in_specs, out_specs=out_specs, check_vma=False)
```

time: 2390 us -> 106 us (0.04)
  the two profiles are of different devices: /device:TPU:8 before, /device:TPU:1 now
where the time goes in v1:
time: 106 us
  Pallas kernels  103 us (97%)
  local copies, waits for them, and re-layouts  2.6 us (2%)
    pallas_call x1, Pallas kernels, body(): pl.pallas_call(kernel, out_shape=(jax.ShapeDtypeStruct((9, 128), F32), ja...  103 us
    unnamed x7, local copies, waits for them, and re-layouts  2.6 us

profile of v1, /device:TPU:1, one launch (start us, length us, event | category | flops | bytes accessed | tf_op | source)
XLA Modules:
  0.0 105.8 jit_solution(14503933542270033360)
XLA Ops:
  0.6 102.6 %schur_cg.1 = (f32[9,128]{1,0:T(8,128)}, f32[9,128]{1,0:T(8,128)}, f32[3,512]{1,0:T(4,128)}) custom-call(f32[2,9,8,512]{3,2,1,0:T(8,128)} %cj.1, f32[2,3,8,512]{3,2,1,0:T(8,128)} %lj.1, f32[2,8,512]{2,1,0:T(8,128)} %rs.1, s32[8,512]{1,0:T(8,128)} %ci.1), custom_call_target="tpu_custom_call" | custom-call | tf_op jit(solution)/shard_map/schur_cg/pallas_call | solution.py:332
  103.2 0.0 copy-start.1
  103.2 1.3 %copy.10 = f32[9,128]{1,0:T(8,128)} copy(f32[9,128]{1,0:T(8,128)} %get-tuple-element.6) | data formatting | bytes 9216
  104.5 0.0 copy-done.1
  104.5 0.0 copy-start
  104.5 0.6 copy.11
  105.1 0.1 copy-done
  105.2 0.6 copy.12
Async XLA Ops:
  103.2 1.3 %copy-start.1 = (f32[9,128]{1,0:T(8,128)S(1)}, f32[9,128]{1,0:T(8,128)}, u32[]{:S(2)}) copy-start(f32[9,128]{1,0:T(8,128)} %get-tuple-element.7) | copy-start | bytes 13828
  104.5 0.7 copy-start

commit v2 on v1

v2 whole, which is shorter than its diff:
```python
import functools

import jax
import jax.numpy as jnp
from jax import lax
from jax.experimental import pallas as pl
from jax.experimental.pallas import tpu as pltpu
from jax.sharding import PartitionSpec as P

DAMPING = 1.0
MESH = pl.DeviceIdType.MESH
F32 = jnp.float32
BF16 = jnp.bfloat16

TILE = 20
K = 8
LM = 512
OBS = K * LM
FLOWS = 4


def split(value):
    high = value.astype(BF16).astype(F32)
    return high, value - high


def rows_sum(value):
    return jnp.sum(value, axis=0, keepdims=True)


def total(buf, count):
    out = buf[0]
    for k in range(1, count):
        out = out + buf[k]
    return out


def kernel(cj_hbm, lj_hbm, rs_hbm, ci_hbm, step_o, res_o, lm_o,
           cj, lj, rs, ci, onehot, tag8, tag16, hot_q, both_sc, last_sc, lhs, fld, acc, last_acc, nat, first_a, err, inv, q_sc,
           terms, cores, plane_buf, pair_buf, even_buf, z_buf, slice_out, slice_in, fields, packed, fin,
           s_core, r_core, s_xy, r_xy, s_zp, r_zp, s_ze, r_ze, s_z, r_z, s_gx, r_gx, s_gc, r_gc, s_fin, r_fin, s_in):
    group = lax.axis_index("group")
    dev = lax.axis_index("dev")
    x, c = group // 2, group % 2
    z, y = dev // 4, dev % 4
    xy = x * 4 + y

    def at(xx, cc, yy, zz):
        return {"group": xx * 2 + cc, "dev": zz * 4 + yy}

    sibling = at(x, 1 - c, y, z)
    plane = []
    for k in (10, 6, 14, 9, 11, 2, 8, 5, 7, 13, 15, 1, 3, 4, 12):
        xx, yy = (x + k // 4) % 4, (y + k % 4) % 4
        plane.append((xx * 4 + yy, at(xx, c, yy, z)))
    pair = z // 2 * 2 + 1 - z % 2
    column = [((z + k) % 16, at(x, c, y, (z + k) % 16)) for k in (8, 7, 9, 6, 10, 5, 11, 4, 12, 3, 13, 2, 14, 1, 15)]
    evens = [((z + k) % 16 // 2, at(x, c, y, (z + k) % 16)) for k in (8, 6, 10, 4, 12, 2, 14)]
    family, cousins = [], []
    for k in (2, 1, 3, 0):
        for o in (1, 0):
            if k or o:
                xx, cc = (x + k) % 4, (c + o) % 2
                family.append((xx * 2 + cc, at(xx, cc, y, z)))
                if k and o:
                    cousins.append(at(xx, cc, y, z))

    barrier = pltpu.get_barrier_semaphore()
    others = [d for _, d in column + plane] + cousins + [sibling]
    for d in others:
        pl.semaphore_signal(barrier, inc=1, device_id=d, device_id_type=MESH)

    loads = [pltpu.make_async_copy(a, b, s_in.at[i])
             for i, (a, b) in enumerate(((ci_hbm, ci), (lj_hbm, lj), (rs_hbm, rs), (cj_hbm, cj)))]
    for load in loads:
        load.start()
    loads[0].wait()

    iota256 = lax.broadcasted_iota(jnp.int32, (256, LM), 0)
    iota32 = lax.broadcasted_iota(jnp.int32, (32, LM), 0)
    for k in range(K):
        ks = pl.ds(k * LM, LM)
        cam = ci[k:k + 1, :]
        low = (cam >> 9) * 16 + (cam & 15)
        tag = (((cam >> 4) & 1) ^ c) * 16 + ((cam >> 5) & 3) * 4 + ((cam >> 7) & 3)
        onehot[:, ks] = jnp.where(iota256 == low, 1.0, 0.0).astype(BF16)
        hot_q[:, ks] = jnp.where(iota32 == tag, 1.0, 0.0).astype(BF16)
        tag8[:, ks] = jnp.broadcast_to(tag, (8, LM))
        tag16[:, ks] = jnp.broadcast_to(tag.astype(F32), (16, LM)).astype(BF16)

    def prepare(k, first8, last):
        ks = pl.ds(k * LM, LM)
        both_sc[:, ks] = jnp.concatenate(split(first8), axis=0).astype(BF16)
        high, low = split(last)
        last_sc[0:1, ks] = high
        last_sc[1:2, ks] = low

    def put_half(base, h):
        for k in range(K):
            ks = pl.ds(k * LM, LM)
            both = both_sc[:, ks]
            tags = tag16[:, ks]
            row = base + h * 288
            for q in range(16):
                lhs[row + q * 16:row + q * 16 + 16, ks] = jnp.where(tags == BF16(h * 16 + q), both, BF16(0))
            hot = hot_q[h * 16:h * 16 + 16, ks]
            lhs[row + 256:row + 272, ks] = hot * jnp.broadcast_to(last_sc[0:1, ks], (16, LM)).astype(BF16)
            lhs[row + 272:row + 288, ks] = hot * jnp.broadcast_to(last_sc[1:2, ks], (16, LM)).astype(BF16)

    def dot_t(left, right):
        return lax.dot_general(left, right, (((1,), (1,)), ((), ())), preferred_element_type=F32)

    iota_rows = lax.broadcasted_iota(jnp.int32, (8, 128), 0)
    lane = lax.broadcasted_iota(jnp.int32, (8, 128), 1)

    def scatter_half(n, base, h, scalar):
        put_half(base, h)
        out = dot_t(lhs[base + h * 288:base + h * 288 + 288, :], onehot[...])
        last = out[256:272] + out[272:288]
        for q in range(16):
            both = out[q * 16:q * 16 + 8] + out[q * 16 + 8:q * 16 + 16]
            terms[n, h, q, 0:8, :] = both[:, 0:128]
            terms[n, h, q, 8:16, :] = both[:, 128:256]
            tail = jnp.where(
                iota_rows == 0, last[q:q + 1, 0:128], jnp.where(
                    iota_rows == 1, last[q:q + 1, 128:256], jnp.where(iota_rows == 2, scalar, 0.0)))
            terms[n, h, q, 16:20, :] = tail[0:4]

    copies = []

    def push(src, dst, send, recv, device):
        copy = pltpu.make_async_remote_copy(
            src_ref=src, dst_ref=dst, send_sem=send, recv_sem=recv, device_id=device, device_id_type=MESH)
        copy.start()
        copies.append(copy)

    def drain(keep):
        while len(copies) > keep:
            copies.pop(0).wait_send()

    def landed(dst, sem):
        pltpu.make_async_copy(dst, dst, sem).wait()

    def start_core(n):
        for i, slot in enumerate([s for s, _ in plane] + [xy]):
            push(terms.at[n, 1, slot], cores.at[n, slot], s_core.at[n, i], r_core.at[n, slot], sibling)

    def start_plane(n):
        for i, (slot, device) in enumerate(plane):
            landed(cores.at[n, slot], r_core.at[n, slot])
            terms[n, 0, slot] = terms[n, 0, slot] + cores[n, slot]
            push(terms.at[n, 0, slot], plane_buf.at[n, xy], s_xy.at[n, i], r_xy.at[n, xy], device)
        landed(cores.at[n, xy], r_core.at[n, xy])
        plane_buf[n, xy] = terms[n, 0, xy] + cores[n, xy]

    def end_plane(n):
        for slot, _ in plane[::-1]:
            landed(plane_buf.at[n, slot], r_xy.at[n, slot])
        return total(plane_buf.at[n], 16)

    def start_gather(n, tile):
        fields[n, 0, xy] = tile
        for i, (slot, device) in enumerate(plane):
            push(fields.at[n, 0, xy], fields.at[n, 0, xy], s_gx.at[n, i], r_gx.at[n, xy], device)
        push(fields.at[n, 0, xy], fields.at[n, 1, xy], s_gc.at[n, 15], r_gc.at[n, xy], sibling)
        for i, (slot, _) in enumerate(plane[::-1]):
            landed(fields.at[n, 0, slot], r_gx.at[n, slot])
            push(fields.at[n, 0, slot], fields.at[n, 1, slot], s_gc.at[n, i], r_gc.at[n, slot], sibling)

    def end_gather(n):
        for slot in [xy] + [s for s, _ in plane[::-1]]:
            landed(fields.at[n, 1, slot], r_gc.at[n, slot])

    def entry(first, second):
        return rows_sum(lj[0, first] * lj[0, second] + lj[1, first] * lj[1, second])

    loads[1].wait()
    loads[2].wait()
    loads[3].wait()
    w_00 = entry(0, 0) + DAMPING
    w_11 = entry(1, 1) + DAMPING
    w_22 = entry(2, 2) + DAMPING
    w_01 = entry(0, 1)
    w_02 = entry(0, 2)
    w_12 = entry(1, 2)
    cof_00 = w_11 * w_22 - w_12 * w_12
    cof_01 = w_02 * w_12 - w_01 * w_22
    cof_02 = w_01 * w_12 - w_02 * w_11
    cof_11 = w_00 * w_22 - w_02 * w_02
    cof_12 = w_01 * w_02 - w_00 * w_12
    cof_22 = w_00 * w_11 - w_01 * w_01
    determinant = w_00 * cof_00 + w_01 * cof_01 + w_02 * cof_02
    for i, cof in enumerate((cof_00, cof_01, cof_02, cof_11, cof_12, cof_22)):
        inv[i:i + 1, :] = cof / determinant

    def eliminate(a0, a1, where):
        side = [rows_sum(lj[0, j] * a0 + lj[1, j] * a1) for j in range(3)]
        picks = ((0, 1, 2), (1, 3, 4), (2, 4, 5))
        e0, e1 = a0, a1
        for j in range(3):
            q = sum(inv[p:p + 1, :] * side[m] for m, p in enumerate(picks[j]))
            q_sc[where * 3 + j:where * 3 + j + 1, :] = q
            e0 = e0 - lj[0, j] * q
            e1 = e1 - lj[1, j] * q
        err[0] = e0
        err[1] = e1
        return e0, e1

    def cam_rows(i, k):
        return cj[i, 0:8, k, :]

    zero = jnp.zeros((1, 128), F32)
    e0, e1 = eliminate(rs[0], rs[1], 0)
    nat[0] = cj[0, 8] * e0 + cj[1, 8] * e1
    nat[1] = cj[0, 8] * cj[0, 8] + cj[1, 8] * cj[1, 8]
    for k in range(K):
        prepare(k, cam_rows(0, k) * err[0, k:k + 1, :] + cam_rows(1, k) * err[1, k:k + 1, :], nat[0, k:k + 1, :])
    scatter_half(0, 0, 1, zero)
    pl.semaphore_wait(barrier, len(others))
    start_core(0)
    scatter_half(0, 0, 0, zero)
    for k in range(K):
        c0, c1 = cam_rows(0, k), cam_rows(1, k)
        prepare(k, c0 * c0 + c1 * c1, nat[1, k:k + 1, :])
    scatter_half(1, 576, 1, zero)
    start_core(1)
    start_plane(0)
    scatter_half(1, 576, 0, zero)
    start_plane(1)

    for n in range(2):
        pair_buf[n, z % 2] = end_plane(n)
        push(pair_buf.at[n, z % 2], pair_buf.at[n, z % 2], s_zp.at[n], r_zp.at[n, z % 2], at(x, c, y, pair))
    for n in range(2):
        landed(pair_buf.at[n, pair % 2], r_zp.at[n, pair % 2])
        even_buf[n, z // 2] = total(pair_buf.at[n], 2)
        for i, (slot, device) in enumerate(evens):
            push(even_buf.at[n, z // 2], even_buf.at[n, z // 2], s_ze.at[n, i], r_ze.at[n, z // 2], device)
    drain(2 * len(evens))
    for n in range(2):
        for slot, _ in evens:
            landed(even_buf.at[n, slot], r_ze.at[n, slot])
    summed = [total(even_buf.at[n], 8) for n in range(2)]
    real = lax.broadcasted_iota(jnp.int32, (TILE, 128), 0) < 18
    scalar_row = lax.broadcasted_iota(jnp.int32, (TILE, 128), 0) == 18

    def inner(left, right):
        return jnp.sum(jnp.where(real, left * right, 0.0), keepdims=True)

    residual = jnp.where(real, summed[0], 0.0)
    diagonal = jnp.where(real, summed[1], 0.0) + DAMPING
    precond = residual / diagonal

    def rz_half(n, h):
        out = fields[n, h, 0, 18:19, :]
        for s in range(1, 16):
            out = out + fields[n, h, s, 18:19, :]
        return out

    def load_half(n, h):
        for s in range(16):
            part = fields[n, h, s]
            h0, l0 = split(part[0:8])
            h1, l1 = split(part[8:16])
            row = h * 288 + s * 16
            fld[row:row + 16, 0:128] = jnp.concatenate([h0, l0], axis=0).astype(BF16)
            fld[row:row + 16, 128:256] = jnp.concatenate([h1, l1], axis=0).astype(BF16)
        for b in range(2):
            high, low = split(fields[n, h, :, 16 + b, :])
            fld[h * 288 + 256:h * 288 + 272, b * 128:b * 128 + 128] = high.astype(BF16)
            fld[h * 288 + 272:h * 288 + 288, b * 128:b * 128 + 128] = low.astype(BF16)

    def pick_half(h, k):
        ks = pl.ds(k * LM, LM)
        out = jnp.dot(fld[h * 288:h * 288 + 288, :], onehot[:, ks], preferred_element_type=F32)
        tags = tag8[:, ks]
        if h:
            high, low = acc[0:8, ks], acc[8:16, ks]
        else:
            high, low = jnp.zeros((8, LM), F32), jnp.zeros((8, LM), F32)
        for s in range(16):
            hit = tags == h * 16 + s
            high = jnp.where(hit, out[s * 16:s * 16 + 8], high)
            low = jnp.where(hit, out[s * 16 + 8:s * 16 + 16], low)
        last = (out[256:272] + out[272:288]) * hot_q[h * 16:h * 16 + 16, ks].astype(F32)
        return high, low, last[0:8] + last[8:16]

    def apply(n, where, wait, flow):
        load_half(n, 0)
        for k in range(K):
            ks = pl.ds(k * LM, LM)
            high, low, last = pick_half(0, k)
            acc[0:8, ks] = high
            acc[8:16, ks] = low
            last_acc[:, ks] = last
        wait()
        load_half(n, 1)
        for k in range(K):
            high, low, last = pick_half(1, k)
            values = high + low
            for i in range(2):
                nat[i, k:k + 1, :] = rows_sum(cam_rows(i, k) * values)
            nat[2, k:k + 1, :] = rows_sum(last + last_acc[:, pl.ds(k * LM, LM)])
        a0 = nat[0] + cj[0, 8] * nat[2]
        a1 = nat[1] + cj[1, 8] * nat[2]
        if n:
            beta = jnp.concatenate([(rz_half(1, 0) + rz_half(1, 1)) / (rz_half(0, 0) + rz_half(0, 1))] * 4, axis=1)
            a0 = a0 + beta * first_a[0]
            a1 = a1 + beta * first_a[1]
        else:
            first_a[0] = a0
            first_a[1] = a1
        e0, e1 = eliminate(a0, a1, where)
        nat[0] = cj[0, 8] * e0 + cj[1, 8] * e1
        product = jnp.sum(a0 * e0 + a1 * e1, keepdims=True)
        for k in range(K):
            prepare(k, cam_rows(0, k) * err[0, k:k + 1, :] + cam_rows(1, k) * err[1, k:k + 1, :], nat[0, k:k + 1, :])
        product = jnp.broadcast_to(product, (1, 128))
        scatter_half(flow, 0, 1, product)
        start_core(flow)
        scatter_half(flow, 0, 0, product)
        start_plane(flow)

    start_gather(0, jnp.where(scalar_row, inner(residual, precond), precond))
    apply(0, 1, lambda: end_gather(0), 2)
    rz = rz_half(0, 0) + rz_half(0, 1)

    def square_half(h, scale):
        out = jnp.zeros((TILE, 128), F32)
        for s in range(16):
            part = fields[0, h, s] if scale is None else fields[1, h, s] + scale * fields[0, h, s]
            out = out + part * part
        return jnp.sum(jnp.where(real, out, 0.0), keepdims=True)

    square = square_half(0, None) + square_half(1, None)
    z_buf[z] = end_plane(2)
    for i, (slot, device) in enumerate(column):
        push(z_buf.at[z], z_buf.at[z], s_z.at[0, i], r_z.at[0, z], device)
    drain(len(column))
    direction = jnp.where(real, fields[0, 0, xy], 0.0)
    for slot, _ in column:
        landed(z_buf.at[slot], r_z.at[0, slot])
    image = total(z_buf, 16)
    alpha1 = rz / (image[18:19] + DAMPING * square)
    residual = residual - alpha1 * jnp.where(real, image + DAMPING * direction, 0.0)
    precond = residual / diagonal
    start_gather(1, jnp.where(scalar_row, inner(residual, precond), precond))

    apply(1, 2, lambda: end_gather(1), 3)
    rz_next = rz_half(1, 0) + rz_half(1, 1)
    beta = rz_next / rz

    square = square_half(0, beta) + square_half(1, beta)

    def swap(value):
        out = value
        for d in range(1, 8):
            moved = pltpu.roll(pltpu.roll(value, 16 * d, 1), 8 - d, 0)
            out = jnp.where((lane // 16 - iota_rows + 8) % 8 == d, moved, out)
        return out

    def pack(store, tile, scalar):
        for b in range(2):
            first = swap(tile[b * 8:b * 8 + 8])
            row = jnp.broadcast_to(tile[16 + b:17 + b], (8, 128))
            second = row
            for g in range(1, 8):
                second = jnp.where(iota_rows == g, pltpu.roll(row, 128 - 16 * g, 1), second)
            second = jnp.where(lane < 16, second, scalar)
            for g in range(8):
                store[b * 8 + g, 0:1, :] = first[g:g + 1]
                store[b * 8 + g, 1:2, :] = second[g:g + 1]

    direction2 = jnp.where(real, fields[1, 0, xy] + beta * direction, 0.0)
    for i, tile in enumerate((direction, direction2, residual)):
        pack(packed.at[i], tile, 0.0)

    own = end_plane(3)
    pack(slice_out, own, jnp.broadcast_to(own[18:19], (8, 128)))
    for i, (slot, device) in enumerate(column):
        push(slice_out.at[slot], slice_in.at[z], s_z.at[1, i], r_z.at[1, z], device)
    slice_in[z] = slice_out[z]
    drain(len(column))
    for slot, _ in column:
        landed(slice_in.at[slot], r_z.at[1, slot])
    image = total(slice_in, 16)
    pick = lax.broadcasted_iota(jnp.int32, (2, 128), 0) * 128 + lax.broadcasted_iota(jnp.int32, (2, 128), 1)
    product = jnp.sum(jnp.where(pick == 144, image, 0.0), keepdims=True)
    alpha2 = rz_next / (product + DAMPING * square)
    fin[group, 0:2, :] = alpha1 * packed[0, z] + alpha2 * packed[1, z]
    fin[group, 2:4, :] = packed[2, z] - alpha2 * (image + DAMPING * packed[1, z])

    for i, (slot, device) in enumerate(family):
        push(fin.at[group], fin.at[group], s_fin.at[i], r_fin.at[group], device)

    scale1 = jnp.concatenate([alpha1] * 4, axis=1)
    scale2 = jnp.concatenate([alpha2] * 4, axis=1)
    lm_o[...] = q_sc[0:3, :] - scale1 * q_sc[3:6, :] - scale2 * q_sc[6:9, :]
    drain(len(family))

    for slot, _ in family:
        landed(fin.at[slot], r_fin.at[slot])
    for i, out in enumerate((step_o, res_o)):
        out[0:8, :] = swap(fin[:, 2 * i, :])
        second = fin[:, 2 * i + 1, :]
        row = second[0:1]
        for g in range(1, 8):
            row = jnp.where(lane[0:1] // 16 == g, pltpu.roll(second, 16 * g, 1)[g:g + 1], row)
        out[8:9, :] = row
    drain(0)


def deliver(step, res, lm, step_o, res_o, lm_o):
    step_o[...] = step[...]
    res_o[...] = res[...]
    lm_o[...] = lm[...]


def body(cam_jac, lm_jac, resid, cam_index):
    vmem = pl.BlockSpec(memory_space=pltpu.VMEM)

    def tiles(*lead):
        return pltpu.VMEM(lead + (TILE, 128), F32)

    dma = pltpu.SemaphoreType.DMA
    scratch = [
        pltpu.VMEM((2, 9, K, LM), F32), pltpu.VMEM((2, 3, K, LM), F32), pltpu.VMEM((2, K, LM), F32), pltpu.VMEM((K, LM), jnp.int32),
        pltpu.VMEM((256, OBS), BF16), pltpu.VMEM((8, OBS), jnp.int32), pltpu.VMEM((16, OBS), BF16), pltpu.VMEM((32, OBS), BF16),
        pltpu.VMEM((16, OBS), BF16), pltpu.VMEM((2, OBS), F32), pltpu.VMEM((1152, OBS), BF16), pltpu.VMEM((576, 256), BF16),
        pltpu.VMEM((16, OBS), F32), pltpu.VMEM((8, OBS), F32),
        pltpu.VMEM((3, K, LM), F32), pltpu.VMEM((2, K, LM), F32), pltpu.VMEM((2, K, LM), F32), pltpu.VMEM((8, LM), F32), pltpu.VMEM((16, LM), F32),
        tiles(FLOWS, 2, 16), tiles(FLOWS, 16), tiles(FLOWS, 16), tiles(2, 2), tiles(2, 8), tiles(16),
        pltpu.VMEM((16, 2, 128), F32), pltpu.VMEM((16, 2, 128), F32), tiles(2, 2, 16), pltpu.VMEM((3, 16, 2, 128), F32),
        pltpu.VMEM((8, 4, 128), F32),
        dma((FLOWS, 16)), dma((FLOWS, 16)), dma((FLOWS, 15)), dma((FLOWS, 16)), dma((2,)), dma((2, 2)), dma((2, 7)), dma((2, 8)),
        dma((2, 15)), dma((2, 16)), dma((2, 15)), dma((2, 16)), dma((2, 16)), dma((2, 16)), dma((7,)), dma((8,)), dma((4,)),
    ]
    out_shape = (jax.ShapeDtypeStruct((9, 128), F32), jax.ShapeDtypeStruct((9, 128), F32), jax.ShapeDtypeStruct((3, LM), F32))
    results = pl.pallas_call(
        kernel,
        out_shape=out_shape,
        in_specs=[pl.BlockSpec(memory_space=pl.ANY)] * 4,
        out_specs=(vmem, vmem, vmem),
        scratch_shapes=scratch,
        name="schur_cg",
        compiler_params=pltpu.CompilerParams(collective_id=0, has_side_effects=True, vmem_limit_bytes=60 << 20),
    )(cam_jac, lm_jac, resid, cam_index)
    return pl.pallas_call(
        deliver,
        out_shape=out_shape,
        in_specs=[vmem] * 3,
        out_specs=(vmem, vmem, vmem),
        name="deliver",
    )(*results)


def solution(mesh):
    in_specs = (
        P(None, None, None, ("group", "dev")),
        P(None, None, None, ("group", "dev")),
        P(None, None, ("group", "dev")),
        P(None, ("group", "dev")),
    )
    out_specs = (P(None, "dev"), P(None, "dev"), P(None, ("group", "dev")))
    return jax.shard_map(body, mesh=mesh, in_specs=in_specs, out_specs=out_specs, check_vma=False)
```

time: 106 us -> 94.7 us (0.89)
  Pallas kernels: 103 us -> 93.8 us
  local copies, waits for them, and re-layouts: 2.6 us -> 0 us
    pallas_call x1 -> x2, Pallas kernels: 103 us -> 93.8 us  [the longest x1 92.4 us: body(): pl.pallas_call(kernel, out_shape=out_shape, in_specs=[pl.BlockSpec(memory...]
    unnamed x7 -> x0, local copies, waits for them, and re-layouts: 2.6 us -> none
where the time goes in v2:
time: 94.7 us; the launch traced here: 94.4 us
  Pallas kernels  93.8 us (99%)
    pallas_call x1, Pallas kernels, body(): pl.pallas_call(kernel, out_shape=out_shape, in_specs=[pl.BlockSpec(memory...  92.4 us

profile of v2, /device:TPU:1, one launch (start us, length us, event | category | flops | bytes accessed | tf_op | source)
XLA Modules:
  0.0 94.4 jit_solution(15548150139708306050)
XLA Ops:
  0.6 92.4 %schur_cg.1 = (f32[9,128]{1,0:T(8,128)}, f32[9,128]{1,0:T(8,128)}, f32[3,512]{1,0:T(4,128)}) custom-call(f32[2,9,8,512]{3,2,1,0:T(8,128)} %cj_hbm.1, f32[2,3,8,512]{3,2,1,0:T(8,128)} %lj_hbm.1, f32[2,8,512]{2,1,0:T(8,128)} %rs_hbm.1, s32[8,512]{1,0:T(8,128)} %ci_hbm.1), custom_call_target="tpu_custom_call" | custom-call | tf_op jit(solution)/shard_map/schur_cg/pallas_call | solution.py:439
  93.1 1.3 %deliver.1 = (f32[9,128]{1,0:T(8,128)}, f32[9,128]{1,0:T(8,128)}, f32[3,512]{1,0:T(4,128)}) custom-call(f32[9,128]{1,0:T(8,128)} %get-tuple-element.6.step, f32[9,128]{1,0:T(8,128)} %get-tuple-element.7.res, f32[3,512]{1,0:T(4,128)} %get-tuple-element.8.lm), custom_call_target="tpu_custom_call" | custom-call | tf_op jit(solution)/shard_map/deliver/pallas_call | solution.py:448

commit v3 on v2

--- a/solution.py
+++ b/solution.py
@@ -126,50 +126,49 @@
                     iota_rows == 1, last[q:q + 1, 128:256], jnp.where(iota_rows == 2, scalar, 0.0)))
             terms[n, h, q, 16:20, :] = tail[0:4]
 
-    copies = []
+    pending = []
 
     def push(src, dst, send, recv, device):
-        copy = pltpu.make_async_remote_copy(
-            src_ref=src, dst_ref=dst, send_sem=send, recv_sem=recv, device_id=device, device_id_type=MESH)
-        copy.start()
-        copies.append(copy)
-
-    def drain(keep):
-        while len(copies) > keep:
-            copies.pop(0).wait_send()
+        pltpu.make_async_remote_copy(
+            src_ref=src, dst_ref=dst, send_sem=send, recv_sem=recv, device_id=device, device_id_type=MESH).start()
 
     def landed(dst, sem):
         pltpu.make_async_copy(dst, dst, sem).wait()
 
+    def drain():
+        while pending:
+            landed(*pending.pop(0))
+
     def start_core(n):
-        for i, slot in enumerate([s for s, _ in plane] + [xy]):
-            push(terms.at[n, 1, slot], cores.at[n, slot], s_core.at[n, i], r_core.at[n, slot], sibling)
+        push(terms.at[n, 1], cores.at[n], s_core.at[n], r_core.at[n], sibling)
+        pending.append((terms.at[n, 1], s_core.at[n]))
 
     def start_plane(n):
-        for i, (slot, device) in enumerate(plane):
-            landed(cores.at[n, slot], r_core.at[n, slot])
+        landed(cores.at[n], r_core.at[n])
+        for slot in range(16):
             terms[n, 0, slot] = terms[n, 0, slot] + cores[n, slot]
-            push(terms.at[n, 0, slot], plane_buf.at[n, xy], s_xy.at[n, i], r_xy.at[n, xy], device)
-        landed(cores.at[n, xy], r_core.at[n, xy])
-        plane_buf[n, xy] = terms[n, 0, xy] + cores[n, xy]
+        for slot, device in plane:
+            push(terms.at[n, 0, slot], plane_buf.at[n, xy], s_xy.at[n], r_xy.at[n], device)
+        pending.append((plane_buf.at[n, pl.ds(0, 15)], s_xy.at[n]))
+        plane_buf[n, xy] = terms[n, 0, xy]
 
     def end_plane(n):
-        for slot, _ in plane[::-1]:
-            landed(plane_buf.at[n, slot], r_xy.at[n, slot])
+        landed(plane_buf.at[n, pl.ds(0, 15)], r_xy.at[n])
         return total(plane_buf.at[n], 16)
 
     def start_gather(n, tile):
         fields[n, 0, xy] = tile
-        for i, (slot, device) in enumerate(plane):
-            push(fields.at[n, 0, xy], fields.at[n, 0, xy], s_gx.at[n, i], r_gx.at[n, xy], device)
-        push(fields.at[n, 0, xy], fields.at[n, 1, xy], s_gc.at[n, 15], r_gc.at[n, xy], sibling)
-        for i, (slot, _) in enumerate(plane[::-1]):
+        for slot, device in plane:
+            push(fields.at[n, 0, xy], fields.at[n, 0, xy], s_gx.at[n], r_gx.at[n, xy], device)
+        pending.append((fields.at[n, 0, pl.ds(0, 15)], s_gx.at[n]))
+        push(fields.at[n, 0, xy], fields.at[n, 1, xy], s_gc.at[n], r_gc.at[n], sibling)
+        for slot, _ in plane[::-1]:
             landed(fields.at[n, 0, slot], r_gx.at[n, slot])
-            push(fields.at[n, 0, slot], fields.at[n, 1, slot], s_gc.at[n, i], r_gc.at[n, slot], sibling)
+            push(fields.at[n, 0, slot], fields.at[n, 1, slot], s_gc.at[n], r_gc.at[n], sibling)
+        pending.append((fields.at[n, 0], s_gc.at[n]))
 
     def end_gather(n):
-        for slot in [xy] + [s for s, _ in plane[::-1]]:
-            landed(fields.at[n, 1, slot], r_gc.at[n, slot])
+        landed(fields.at[n, 1], r_gc.at[n])
 
     def entry(first, second):
         return rows_sum(lj[0, first] * lj[0, second] + lj[1, first] * lj[1, second])
@@ -230,16 +229,17 @@
 
     for n in range(2):
         pair_buf[n, z % 2] = end_plane(n)
-        push(pair_buf.at[n, z % 2], pair_buf.at[n, z % 2], s_zp.at[n], r_zp.at[n, z % 2], at(x, c, y, pair))
+        push(pair_buf.at[n, z % 2], pair_buf.at[n, z % 2], s_zp.at[n], r_zp.at[n], at(x, c, y, pair))
+        pending.append((pair_buf.at[n, 0], s_zp.at[n]))
     for n in range(2):
-        landed(pair_buf.at[n, pair % 2], r_zp.at[n, pair % 2])
+        landed(pair_buf.at[n, pair % 2], r_zp.at[n])
         even_buf[n, z // 2] = total(pair_buf.at[n], 2)
-        for i, (slot, device) in enumerate(evens):
-            push(even_buf.at[n, z // 2], even_buf.at[n, z // 2], s_ze.at[n, i], r_ze.at[n, z // 2], device)
-    drain(2 * len(evens))
+        for _, device in evens:
+            push(even_buf.at[n, z // 2], even_buf.at[n, z // 2], s_ze.at[n], r_ze.at[n], device)
+    drain()
     for n in range(2):
-        for slot, _ in evens:
-            landed(even_buf.at[n, slot], r_ze.at[n, slot])
+        landed(even_buf.at[n, pl.ds(0, 7)], r_ze.at[n])
+        pending.append((even_buf.at[n, pl.ds(0, 7)], s_ze.at[n]))
     summed = [total(even_buf.at[n], 8) for n in range(2)]
     real = lax.broadcasted_iota(jnp.int32, (TILE, 128), 0) < 18
     scalar_row = lax.broadcasted_iota(jnp.int32, (TILE, 128), 0) == 18
@@ -334,12 +334,12 @@
 
     square = square_half(0, None) + square_half(1, None)
     z_buf[z] = end_plane(2)
-    for i, (slot, device) in enumerate(column):
-        push(z_buf.at[z], z_buf.at[z], s_z.at[0, i], r_z.at[0, z], device)
-    drain(len(column))
+    for _, device in column:
+        push(z_buf.at[z], z_buf.at[z], s_z.at[0], r_z.at[0], device)
+    drain()
     direction = jnp.where(real, fields[0, 0, xy], 0.0)
-    for slot, _ in column:
-        landed(z_buf.at[slot], r_z.at[0, slot])
+    landed(z_buf.at[pl.ds(0, 15)], r_z.at[0])
+    pending.append((z_buf.at[pl.ds(0, 15)], s_z.at[0]))
     image = total(z_buf, 16)
     alpha1 = rz / (image[18:19] + DAMPING * square)
     residual = residual - alpha1 * jnp.where(real, image + DAMPING * direction, 0.0)
@@ -377,12 +377,11 @@
 
     own = end_plane(3)
     pack(slice_out, own, jnp.broadcast_to(own[18:19], (8, 128)))
-    for i, (slot, device) in enumerate(column):
-        push(slice_out.at[slot], slice_in.at[z], s_z.at[1, i], r_z.at[1, z], device)
+    for slot, device in column:
+        push(slice_out.at[slot], slice_in.at[z], s_z.at[1], r_z.at[1], device)
     slice_in[z] = slice_out[z]
-    drain(len(column))
-    for slot, _ in column:
-        landed(slice_in.at[slot], r_z.at[1, slot])
+    drain()
+    landed(slice_in.at[pl.ds(0, 15)], r_z.at[1])
     image = total(slice_in, 16)
     pick = lax.broadcasted_iota(jnp.int32, (2, 128), 0) * 128 + lax.broadcasted_iota(jnp.int32, (2, 128), 1)
     product = jnp.sum(jnp.where(pick == 144, image, 0.0), keepdims=True)
@@ -390,16 +389,14 @@
     fin[group, 0:2, :] = alpha1 * packed[0, z] + alpha2 * packed[1, z]
     fin[group, 2:4, :] = packed[2, z] - alpha2 * (image + DAMPING * packed[1, z])
 
-    for i, (slot, device) in enumerate(family):
-        push(fin.at[group], fin.at[group], s_fin.at[i], r_fin.at[group], device)
+    for _, device in family:
+        push(fin.at[group], fin.at[group], s_fin.at[0], r_fin.at[0], device)
+    landed(slice_in.at[pl.ds(0, 15)], s_z.at[1])
 
     scale1 = jnp.concatenate([alpha1] * 4, axis=1)
     scale2 = jnp.concatenate([alpha2] * 4, axis=1)
     lm_o[...] = q_sc[0:3, :] - scale1 * q_sc[3:6, :] - scale2 * q_sc[6:9, :]
-    drain(len(family))
-
-    for slot, _ in family:
-        landed(fin.at[slot], r_fin.at[slot])
+    landed(fin.at[pl.ds(0, 7)], r_fin.at[0])
     for i, out in enumerate((step_o, res_o)):
         out[0:8, :] = swap(fin[:, 2 * i, :])
         second = fin[:, 2 * i + 1, :]
@@ -407,7 +404,7 @@
         for g in range(1, 8):
             row = jnp.where(lane[0:1] // 16 == g, pltpu.roll(second, 16 * g, 1)[g:g + 1], row)
         out[8:9, :] = row
-    drain(0)
+    landed(fin.at[pl.ds(0, 7)], s_fin.at[0])
 
 
 def deliver(step, res, lm, step_o, res_o, lm_o):
@@ -432,13 +429,13 @@
         tiles(FLOWS, 2, 16), tiles(FLOWS, 16), tiles(FLOWS, 16), tiles(2, 2), tiles(2, 8), tiles(16),
         pltpu.VMEM((16, 2, 128), F32), pltpu.VMEM((16, 2, 128), F32), tiles(2, 2, 16), pltpu.VMEM((3, 16, 2, 128), F32),
         pltpu.VMEM((8, 4, 128), F32),
-        dma((FLOWS, 16)), dma((FLOWS, 16)), dma((FLOWS, 15)), dma((FLOWS, 16)), dma((2,)), dma((2, 2)), dma((2, 7)), dma((2, 8)),
-        dma((2, 15)), dma((2, 16)), dma((2, 15)), dma((2, 16)), dma((2, 16)), dma((2, 16)), dma((7,)), dma((8,)), dma((4,)),
+        dma((FLOWS,)), dma((FLOWS,)), dma((FLOWS,)), dma((FLOWS,)), dma((2,)), dma((2,)), dma((2,)), dma((2,)),
+        dma((2,)), dma((2,)), dma((2,)), dma((2, 16)), dma((2,)), dma((2,)), dma((1,)), dma((1,)), dma((4,)),
     ]
     out_shape = (jax.ShapeDtypeStruct((9, 128), F32), jax.ShapeDtypeStruct((9, 128), F32), jax.ShapeDtypeStruct((3, LM), F32))
     results = pl.pallas_call(
         kernel,
-        out_shape=out_shape,
+        out_shape=(pltpu.VMEM((9, 128), F32), pltpu.VMEM((9, 128), F32), pltpu.VMEM((3, LM), F32)),
         in_specs=[pl.BlockSpec(memory_space=pl.ANY)] * 4,
         out_specs=(vmem, vmem, vmem),
         scratch_shapes=scratch,
@@ -451,7 +448,7 @@
         in_specs=[vmem] * 3,
         out_specs=(vmem, vmem, vmem),
         name="deliver",
-    )(*results)
+    )(*(pltpu.with_memory_space_constraint(r, pltpu.MemorySpace.VMEM) for r in results))
 
 
 def solution(mesh):

time: 94.7 us -> 89.1 us (0.941)
  Pallas kernels: 93.8 us -> 88.3 us
    pallas_call x1, Pallas kernels: 92.4 us -> 87.7 us  [body(): pl.pallas_call(kernel, out_shape=(pltpu.VMEM((9, 128), F32), pltpu.VMEM((...]
where the time goes in v3:
time: 89.1 us; the launch traced here: 88.9 us
  Pallas kernels  88.3 us (99%)
    pallas_call x1, Pallas kernels, body(): pl.pallas_call(kernel, out_shape=(pltpu.VMEM((9, 128), F32), pltpu.VMEM((...  87.7 us

profile of v3, /device:TPU:1, one launch (start us, length us, event | category | flops | bytes accessed | tf_op | source)
XLA Modules:
  0.0 88.9 jit_solution(13302798072759631648)
XLA Ops:
  0.6 87.7 %schur_cg.1 = (f32[9,128]{1,0:T(8,128)S(1)}, f32[9,128]{1,0:T(8,128)S(1)}, f32[3,512]{1,0:T(4,128)S(1)}) custom-call(f32[2,9,8,512]{3,2,1,0:T(8,128)} %cj_hbm.1, f32[2,3,8,512]{3,2,1,0:T(8,128)} %lj_hbm.1, f32[2,8,512]{2,1,0:T(8,128)} %rs_hbm.1, s32[8,512]{1,0:T(8,128)} %ci_hbm.1), custom_call_target="tpu_custom_call" | custom-call | tf_op jit(solution)/shard_map/schur_cg/pallas_call | solution.py:436
  88.3 0.6 deliver.1

commit v4 on v3

--- a/solution.py
+++ b/solution.py
@@ -12,11 +12,11 @@
 F32 = jnp.float32
 BF16 = jnp.bfloat16
 
-TILE = 20
+TILE = 10
 K = 8
 LM = 512
 OBS = K * LM
-FLOWS = 4
+FLOWS = 3
 
 
 def split(value):
@@ -37,8 +37,8 @@
 
 def kernel(cj_hbm, lj_hbm, rs_hbm, ci_hbm, step_o, res_o, lm_o,
            cj, lj, rs, ci, onehot, tag8, tag16, hot_q, both_sc, last_sc, lhs, fld, acc, last_acc, nat, first_a, err, inv, q_sc,
-           terms, cores, plane_buf, pair_buf, even_buf, z_buf, slice_out, slice_in, fields, packed, fin,
-           s_core, r_core, s_xy, r_xy, s_zp, r_zp, s_ze, r_ze, s_z, r_z, s_gx, r_gx, s_gc, r_gc, s_fin, r_fin, s_in):
+           terms, cores, plane_buf, terms1, cores1, plane1, even1, even2, slice_out, slice_in, fields, packed, fin,
+           s_core, r_core, s_xy, r_xy, s_ze, r_ze, s_z, r_z, s_gx, r_gx, s_gc, r_gc, s_fin, r_fin, s_in):
     group = lax.axis_index("group")
     dev = lax.axis_index("dev")
     x, c = group // 2, group % 2
@@ -49,13 +49,16 @@
         return {"group": xx * 2 + cc, "dev": zz * 4 + yy}
 
     sibling = at(x, 1 - c, y, z)
+    odd, level = z % 2, z // 2
+    mine = odd * 16 + xy
     plane = []
-    for k in (10, 6, 14, 9, 11, 2, 8, 5, 7, 13, 15, 1, 3, 4, 12):
+    for k in (10, 6, 14, 9, 11, 2, 8, 5, 7, 13, 15, 1, 3, 4, 12, 0):
         xx, yy = (x + k // 4) % 4, (y + k % 4) % 4
-        plane.append((xx * 4 + yy, at(xx, c, yy, z)))
-    pair = z // 2 * 2 + 1 - z % 2
-    column = [((z + k) % 16, at(x, c, y, (z + k) % 16)) for k in (8, 7, 9, 6, 10, 5, 11, 4, 12, 3, 13, 2, 14, 1, 15)]
-    evens = [((z + k) % 16 // 2, at(x, c, y, (z + k) % 16)) for k in (8, 6, 10, 4, 12, 2, 14)]
+        for o in (1, 0):
+            if k or o:
+                b = (odd + o) % 2
+                plane.append((b * 16 + xx * 4 + yy, at(xx, c, yy, level * 2 + b)))
+    evens = [((level + k) % 8, at(x, c, y, (z + 2 * k) % 16)) for k in (4, 3, 5, 2, 6, 1, 7)]
     family, cousins = [], []
     for k in (2, 1, 3, 0):
         for o in (1, 0):
@@ -65,15 +68,16 @@
                 if k and o:
                     cousins.append(at(xx, cc, y, z))
 
-    barrier = pltpu.get_barrier_semaphore()
-    others = [d for _, d in column + plane] + cousins + [sibling]
-    for d in others:
-        pl.semaphore_signal(barrier, inc=1, device_id=d, device_id_type=MESH)
-
     loads = [pltpu.make_async_copy(a, b, s_in.at[i])
              for i, (a, b) in enumerate(((ci_hbm, ci), (lj_hbm, lj), (rs_hbm, rs), (cj_hbm, cj)))]
     for load in loads:
         load.start()
+
+    barrier = pltpu.get_barrier_semaphore()
+    others = [d for _, d in evens + plane] + cousins + [sibling]
+    for d in others:
+        pl.semaphore_signal(barrier, inc=1, device_id=d, device_id_type=MESH)
+
     loads[0].wait()
 
     iota256 = lax.broadcasted_iota(jnp.int32, (256, LM), 0)
@@ -81,7 +85,7 @@
     for k in range(K):
         ks = pl.ds(k * LM, LM)
         cam = ci[k:k + 1, :]
-        low = (cam >> 9) * 16 + (cam & 15)
+        low = ((cam >> 9) & 1) * 128 + (cam >> 10) * 16 + (cam & 15)
         tag = (((cam >> 4) & 1) ^ c) * 16 + ((cam >> 5) & 3) * 4 + ((cam >> 7) & 3)
         onehot[:, ks] = jnp.where(iota256 == low, 1.0, 0.0).astype(BF16)
         hot_q[:, ks] = jnp.where(iota32 == tag, 1.0, 0.0).astype(BF16)
@@ -113,18 +117,16 @@
     iota_rows = lax.broadcasted_iota(jnp.int32, (8, 128), 0)
     lane = lax.broadcasted_iota(jnp.int32, (8, 128), 1)
 
-    def scatter_half(n, base, h, scalar):
+    def scatter_half(out_terms, base, h, scalar):
         put_half(base, h)
         out = dot_t(lhs[base + h * 288:base + h * 288 + 288, :], onehot[...])
         last = out[256:272] + out[272:288]
         for q in range(16):
             both = out[q * 16:q * 16 + 8] + out[q * 16 + 8:q * 16 + 16]
-            terms[n, h, q, 0:8, :] = both[:, 0:128]
-            terms[n, h, q, 8:16, :] = both[:, 128:256]
-            tail = jnp.where(
-                iota_rows == 0, last[q:q + 1, 0:128], jnp.where(
-                    iota_rows == 1, last[q:q + 1, 128:256], jnp.where(iota_rows == 2, scalar, 0.0)))
-            terms[n, h, q, 16:20, :] = tail[0:4]
+            for b in range(2):
+                out_terms(h, b * 16 + q)[0:8, :] = both[:, b * 128:b * 128 + 128]
+                tail = jnp.where(iota_rows == 0, last[q:q + 1, b * 128:b * 128 + 128], scalar)
+                out_terms(h, b * 16 + q)[8:10, :] = tail[0:2]
 
     pending = []
 
@@ -139,32 +141,35 @@
         while pending:
             landed(*pending.pop(0))
 
+    flows = ((terms1, cores1, plane1), (terms.at[0], cores.at[0], plane_buf.at[0]), (terms.at[1], cores.at[1], plane_buf.at[1]))
+
     def start_core(n):
-        push(terms.at[n, 1], cores.at[n], s_core.at[n], r_core.at[n], sibling)
-        pending.append((terms.at[n, 1], s_core.at[n]))
+        source, store, _ = flows[n]
+        push(source.at[1], store, s_core.at[n], r_core.at[n], sibling)
+        pending.append((source.at[1], s_core.at[n]))
 
     def start_plane(n):
-        landed(cores.at[n], r_core.at[n])
-        for slot in range(16):
-            terms[n, 0, slot] = terms[n, 0, slot] + cores[n, slot]
+        source, store, spread = flows[n]
+        landed(store, r_core.at[n])
+        for slot in range(32):
+            source[0, slot] = source[0, slot] + store[slot]
         for slot, device in plane:
-            push(terms.at[n, 0, slot], plane_buf.at[n, xy], s_xy.at[n], r_xy.at[n], device)
-        pending.append((plane_buf.at[n, pl.ds(0, 15)], s_xy.at[n]))
-        plane_buf[n, xy] = terms[n, 0, xy]
+            push(source.at[0, slot], spread.at[mine], s_xy.at[n], r_xy.at[n], device)
+        pending.append((spread.at[pl.ds(0, 31)], s_xy.at[n]))
+        spread[mine] = source[0, mine]
 
     def end_plane(n):
-        landed(plane_buf.at[n, pl.ds(0, 15)], r_xy.at[n])
-        return total(plane_buf.at[n], 16)
+        spread = flows[n][2]
+        landed(spread.at[pl.ds(0, 31)], r_xy.at[n])
+        return total(spread, 32)
 
     def start_gather(n, tile):
-        fields[n, 0, xy] = tile
+        fields[n, 0, mine] = tile
         for slot, device in plane:
-            push(fields.at[n, 0, xy], fields.at[n, 0, xy], s_gx.at[n], r_gx.at[n, xy], device)
-        pending.append((fields.at[n, 0, pl.ds(0, 15)], s_gx.at[n]))
-        push(fields.at[n, 0, xy], fields.at[n, 1, xy], s_gc.at[n], r_gc.at[n], sibling)
-        for slot, _ in plane[::-1]:
-            landed(fields.at[n, 0, slot], r_gx.at[n, slot])
-            push(fields.at[n, 0, slot], fields.at[n, 1, slot], s_gc.at[n], r_gc.at[n], sibling)
+            push(fields.at[n, 0, mine], fields.at[n, 0, mine], s_gx.at[n], r_gx.at[n], device)
+        pending.append((fields.at[n, 0, pl.ds(0, 31)], s_gx.at[n]))
+        landed(fields.at[n, 0, pl.ds(0, 31)], r_gx.at[n])
+        push(fields.at[n, 0], fields.at[n, 1], s_gc.at[n], r_gc.at[n], sibling)
         pending.append((fields.at[n, 0], s_gc.at[n]))
 
     def end_gather(n):
@@ -214,35 +219,26 @@
     nat[1] = cj[0, 8] * cj[0, 8] + cj[1, 8] * cj[1, 8]
     for k in range(K):
         prepare(k, cam_rows(0, k) * err[0, k:k + 1, :] + cam_rows(1, k) * err[1, k:k + 1, :], nat[0, k:k + 1, :])
-    scatter_half(0, 0, 1, zero)
-    pl.semaphore_wait(barrier, len(others))
-    start_core(0)
-    scatter_half(0, 0, 0, zero)
+    scatter_half(lambda h, q: terms1.at[h, q, 0], 0, 1, zero)
+    scatter_half(lambda h, q: terms1.at[h, q, 0], 0, 0, zero)
     for k in range(K):
         c0, c1 = cam_rows(0, k), cam_rows(1, k)
         prepare(k, c0 * c0 + c1 * c1, nat[1, k:k + 1, :])
-    scatter_half(1, 576, 1, zero)
-    start_core(1)
+    scatter_half(lambda h, q: terms1.at[h, q, 1], 576, 1, zero)
+    pl.semaphore_wait(barrier, len(others))
+    start_core(0)
+    scatter_half(lambda h, q: terms1.at[h, q, 1], 576, 0, zero)
     start_plane(0)
-    scatter_half(1, 576, 0, zero)
-    start_plane(1)
-
-    for n in range(2):
-        pair_buf[n, z % 2] = end_plane(n)
-        push(pair_buf.at[n, z % 2], pair_buf.at[n, z % 2], s_zp.at[n], r_zp.at[n], at(x, c, y, pair))
-        pending.append((pair_buf.at[n, 0], s_zp.at[n]))
-    for n in range(2):
-        landed(pair_buf.at[n, pair % 2], r_zp.at[n])
-        even_buf[n, z // 2] = total(pair_buf.at[n], 2)
-        for _, device in evens:
-            push(even_buf.at[n, z // 2], even_buf.at[n, z // 2], s_ze.at[n], r_ze.at[n], device)
+
+    even1[level] = end_plane(0)
+    for _, device in evens:
+        push(even1.at[level], even1.at[level], s_ze.at[0], r_ze.at[0], device)
     drain()
-    for n in range(2):
-        landed(even_buf.at[n, pl.ds(0, 7)], r_ze.at[n])
-        pending.append((even_buf.at[n, pl.ds(0, 7)], s_ze.at[n]))
-    summed = [total(even_buf.at[n], 8) for n in range(2)]
-    real = lax.broadcasted_iota(jnp.int32, (TILE, 128), 0) < 18
-    scalar_row = lax.broadcasted_iota(jnp.int32, (TILE, 128), 0) == 18
+    landed(even1.at[pl.ds(0, 7)], r_ze.at[0])
+    pending.append((even1.at[pl.ds(0, 7)], s_ze.at[0]))
+    summed = total(even1, 8)
+    real = lax.broadcasted_iota(jnp.int32, (TILE, 128), 0) < 9
+    scalar_row = lax.broadcasted_iota(jnp.int32, (TILE, 128), 0) == 9
 
     def inner(left, right):
         return jnp.sum(jnp.where(real, left * right, 0.0), keepdims=True)
@@ -252,21 +248,20 @@
     precond = residual / diagonal
 
     def rz_half(n, h):
-        out = fields[n, h, 0, 18:19, :]
-        for s in range(1, 16):
-            out = out + fields[n, h, s, 18:19, :]
+        out = fields[n, h, 0, 9:10, :]
+        for s in range(1, 32):
+            out = out + fields[n, h, s, 9:10, :]
         return out
 
     def load_half(n, h):
         for s in range(16):
-            part = fields[n, h, s]
-            h0, l0 = split(part[0:8])
-            h1, l1 = split(part[8:16])
+            h0, l0 = split(fields[n, h, s, 0:8, :])
+            h1, l1 = split(fields[n, h, 16 + s, 0:8, :])
             row = h * 288 + s * 16
             fld[row:row + 16, 0:128] = jnp.concatenate([h0, l0], axis=0).astype(BF16)
             fld[row:row + 16, 128:256] = jnp.concatenate([h1, l1], axis=0).astype(BF16)
         for b in range(2):
-            high, low = split(fields[n, h, :, 16 + b, :])
+            high, low = split(fields[n, h, pl.ds(b * 16, 16), 8, :])
             fld[h * 288 + 256:h * 288 + 272, b * 128:b * 128 + 128] = high.astype(BF16)
             fld[h * 288 + 272:h * 288 + 288, b * 128:b * 128 + 128] = low.astype(BF16)
 
@@ -316,37 +311,37 @@
         for k in range(K):
             prepare(k, cam_rows(0, k) * err[0, k:k + 1, :] + cam_rows(1, k) * err[1, k:k + 1, :], nat[0, k:k + 1, :])
         product = jnp.broadcast_to(product, (1, 128))
-        scatter_half(flow, 0, 1, product)
+        scatter_half(lambda h, q: terms.at[flow - 1, h, q], 0, 1, product)
         start_core(flow)
-        scatter_half(flow, 0, 0, product)
+        scatter_half(lambda h, q: terms.at[flow - 1, h, q], 0, 0, product)
         start_plane(flow)
 
     start_gather(0, jnp.where(scalar_row, inner(residual, precond), precond))
-    apply(0, 1, lambda: end_gather(0), 2)
+    apply(0, 1, lambda: end_gather(0), 1)
     rz = rz_half(0, 0) + rz_half(0, 1)
 
     def square_half(h, scale):
         out = jnp.zeros((TILE, 128), F32)
-        for s in range(16):
+        for s in range(32):
             part = fields[0, h, s] if scale is None else fields[1, h, s] + scale * fields[0, h, s]
             out = out + part * part
         return jnp.sum(jnp.where(real, out, 0.0), keepdims=True)
 
     square = square_half(0, None) + square_half(1, None)
-    z_buf[z] = end_plane(2)
-    for _, device in column:
-        push(z_buf.at[z], z_buf.at[z], s_z.at[0], r_z.at[0], device)
+    even2[level] = end_plane(1)
+    for _, device in evens:
+        push(even2.at[level], even2.at[level], s_ze.at[1], r_ze.at[1], device)
     drain()
-    direction = jnp.where(real, fields[0, 0, xy], 0.0)
-    landed(z_buf.at[pl.ds(0, 15)], r_z.at[0])
-    pending.append((z_buf.at[pl.ds(0, 15)], s_z.at[0]))
-    image = total(z_buf, 16)
-    alpha1 = rz / (image[18:19] + DAMPING * square)
+    direction = jnp.where(real, fields[0, 0, mine], 0.0)
+    landed(even2.at[pl.ds(0, 7)], r_ze.at[1])
+    pending.append((even2.at[pl.ds(0, 7)], s_ze.at[1]))
+    image = total(even2, 8)
+    alpha1 = rz / (image[9:10] + DAMPING * square)
     residual = residual - alpha1 * jnp.where(real, image + DAMPING * direction, 0.0)
     precond = residual / diagonal
     start_gather(1, jnp.where(scalar_row, inner(residual, precond), precond))
 
-    apply(1, 2, lambda: end_gather(1), 3)
+    apply(1, 2, lambda: end_gather(1), 2)
     rz_next = rz_half(1, 0) + rz_half(1, 1)
     beta = rz_next / rz
 
@@ -360,38 +355,37 @@
         return out
 
     def pack(store, tile, scalar):
-        for b in range(2):
-            first = swap(tile[b * 8:b * 8 + 8])
-            row = jnp.broadcast_to(tile[16 + b:17 + b], (8, 128))
-            second = row
-            for g in range(1, 8):
-                second = jnp.where(iota_rows == g, pltpu.roll(row, 128 - 16 * g, 1), second)
-            second = jnp.where(lane < 16, second, scalar)
-            for g in range(8):
-                store[b * 8 + g, 0:1, :] = first[g:g + 1]
-                store[b * 8 + g, 1:2, :] = second[g:g + 1]
-
-    direction2 = jnp.where(real, fields[1, 0, xy] + beta * direction, 0.0)
+        first = swap(tile[0:8])
+        row = jnp.broadcast_to(tile[8:9], (8, 128))
+        second = row
+        for g in range(1, 8):
+            second = jnp.where(iota_rows == g, pltpu.roll(row, 128 - 16 * g, 1), second)
+        second = jnp.where(lane < 16, second, scalar)
+        for g in range(8):
+            store[g, 0:1, :] = first[g:g + 1]
+            store[g, 1:2, :] = second[g:g + 1]
+
+    direction2 = jnp.where(real, fields[1, 0, mine] + beta * direction, 0.0)
     for i, tile in enumerate((direction, direction2, residual)):
         pack(packed.at[i], tile, 0.0)
 
-    own = end_plane(3)
-    pack(slice_out, own, jnp.broadcast_to(own[18:19], (8, 128)))
-    for slot, device in column:
-        push(slice_out.at[slot], slice_in.at[z], s_z.at[1], r_z.at[1], device)
-    slice_in[z] = slice_out[z]
+    own = end_plane(2)
+    pack(slice_out, own, jnp.broadcast_to(own[9:10], (8, 128)))
+    for slot, device in evens:
+        push(slice_out.at[slot], slice_in.at[level], s_z.at[0], r_z.at[0], device)
+    slice_in[level] = slice_out[level]
     drain()
-    landed(slice_in.at[pl.ds(0, 15)], r_z.at[1])
-    image = total(slice_in, 16)
+    landed(slice_in.at[pl.ds(0, 7)], r_z.at[0])
+    image = total(slice_in, 8)
     pick = lax.broadcasted_iota(jnp.int32, (2, 128), 0) * 128 + lax.broadcasted_iota(jnp.int32, (2, 128), 1)
     product = jnp.sum(jnp.where(pick == 144, image, 0.0), keepdims=True)
     alpha2 = rz_next / (product + DAMPING * square)
-    fin[group, 0:2, :] = alpha1 * packed[0, z] + alpha2 * packed[1, z]
-    fin[group, 2:4, :] = packed[2, z] - alpha2 * (image + DAMPING * packed[1, z])
+    fin[group, 0:2, :] = alpha1 * packed[0, level] + alpha2 * packed[1, level]
+    fin[group, 2:4, :] = packed[2, level] - alpha2 * (image + DAMPING * packed[1, level])
 
     for _, device in family:
         push(fin.at[group], fin.at[group], s_fin.at[0], r_fin.at[0], device)
-    landed(slice_in.at[pl.ds(0, 15)], s_z.at[1])
+    landed(slice_in.at[pl.ds(0, 7)], s_z.at[0])
 
     scale1 = jnp.concatenate([alpha1] * 4, axis=1)
     scale2 = jnp.concatenate([alpha2] * 4, axis=1)
@@ -426,11 +420,11 @@
         pltpu.VMEM((16, OBS), BF16), pltpu.VMEM((2, OBS), F32), pltpu.VMEM((1152, OBS), BF16), pltpu.VMEM((576, 256), BF16),
         pltpu.VMEM((16, OBS), F32), pltpu.VMEM((8, OBS), F32),
         pltpu.VMEM((3, K, LM), F32), pltpu.VMEM((2, K, LM), F32), pltpu.VMEM((2, K, LM), F32), pltpu.VMEM((8, LM), F32), pltpu.VMEM((16, LM), F32),
-        tiles(FLOWS, 2, 16), tiles(FLOWS, 16), tiles(FLOWS, 16), tiles(2, 2), tiles(2, 8), tiles(16),
-        pltpu.VMEM((16, 2, 128), F32), pltpu.VMEM((16, 2, 128), F32), tiles(2, 2, 16), pltpu.VMEM((3, 16, 2, 128), F32),
+        tiles(2, 2, 32), tiles(2, 32), tiles(2, 32), tiles(2, 32, 2), tiles(32, 2), tiles(32, 2), tiles(8, 2), tiles(8),
+        pltpu.VMEM((8, 2, 128), F32), pltpu.VMEM((8, 2, 128), F32), tiles(2, 2, 32), pltpu.VMEM((3, 8, 2, 128), F32),
         pltpu.VMEM((8, 4, 128), F32),
-        dma((FLOWS,)), dma((FLOWS,)), dma((FLOWS,)), dma((FLOWS,)), dma((2,)), dma((2,)), dma((2,)), dma((2,)),
-        dma((2,)), dma((2,)), dma((2,)), dma((2, 16)), dma((2,)), dma((2,)), dma((1,)), dma((1,)), dma((4,)),
+        dma((FLOWS,)), dma((FLOWS,)), dma((FLOWS,)), dma((FLOWS,)), dma((2,)), dma((2,)), dma((1,)), dma((1,)),
+        dma((2,)), dma((2,)), dma((2,)), dma((2,)), dma((1,)), dma((1,)), dma((4,)),
     ]
     out_shape = (jax.ShapeDtypeStruct((9, 128), F32), jax.ShapeDtypeStruct((9, 128), F32), jax.ShapeDtypeStruct((3, LM), F32))
     results = pl.pallas_call(

time: 89.1 us -> 83 us (0.932)
  Pallas kernels: 88.3 us -> 82.2 us
    pallas_call x1, Pallas kernels: 87.7 us -> 81.6 us  [body(): pl.pallas_call(kernel, out_shape=(pltpu.VMEM((9, 128), F32), pltpu.VMEM((...]
where the time goes in v4:
time: 83 us; the launch traced here: 82.8 us
  Pallas kernels  82.2 us (99%)
    pallas_call x1, Pallas kernels, body(): pl.pallas_call(kernel, out_shape=(pltpu.VMEM((9, 128), F32), pltpu.VMEM((...  81.6 us

profile of v4, /device:TPU:1, one launch (start us, length us, event | category | flops | bytes accessed | tf_op | source)
XLA Modules:
  0.0 82.8 jit_solution(7482764183376464749)
XLA Ops:
  0.6 81.6 %schur_cg.1 = (f32[9,128]{1,0:T(8,128)S(1)}, f32[9,128]{1,0:T(8,128)S(1)}, f32[3,512]{1,0:T(4,128)S(1)}) custom-call(f32[2,9,8,512]{3,2,1,0:T(8,128)} %cj_hbm.1, f32[2,3,8,512]{3,2,1,0:T(8,128)} %lj_hbm.1, f32[2,8,512]{2,1,0:T(8,128)} %rs_hbm.1, s32[8,512]{1,0:T(8,128)} %ci_hbm.1), custom_call_target="tpu_custom_call" | custom-call | tf_op jit(solution)/shard_map/schur_cg/pallas_call | solution.py:430
  82.2 0.6 deliver.1

commit v5 on v4

--- a/solution.py
+++ b/solution.py
@@ -37,8 +37,8 @@
 
 def kernel(cj_hbm, lj_hbm, rs_hbm, ci_hbm, step_o, res_o, lm_o,
            cj, lj, rs, ci, onehot, tag8, tag16, hot_q, both_sc, last_sc, lhs, fld, acc, last_acc, nat, first_a, err, inv, q_sc,
-           terms, cores, plane_buf, terms1, cores1, plane1, even1, even2, slice_out, slice_in, fields, packed, fin,
-           s_core, r_core, s_xy, r_xy, s_ze, r_ze, s_z, r_z, s_gx, r_gx, s_gc, r_gc, s_fin, r_fin, s_in):
+           terms, cores, plane_buf, terms1, cores1, plane1, even1, even2, slice_out, slice_in, fields, packed, known, images, fin,
+           s_core, r_core, s_xy, r_xy, s_ze, r_ze, s_z, r_z, s_gx, r_gx, s_gc, r_gc, s_fin, r_fin, s_img, r_img, s_in):
     group = lax.axis_index("group")
     dev = lax.axis_index("dev")
     x, c = group // 2, group % 2
@@ -59,6 +59,11 @@
                 b = (odd + o) % 2
                 plane.append((b * 16 + xx * 4 + yy, at(xx, c, yy, level * 2 + b)))
     evens = [((level + k) % 8, at(x, c, y, (z + 2 * k) % 16)) for k in (4, 3, 5, 2, 6, 1, 7)]
+    spots = []
+    for k in (4, 3, 5, 2, 6, 1, 7, 0):
+        for q in (2, 1, 3, 0):
+            if k or q:
+                spots.append(((level + k) % 8, at((x + q) % 4, c, y, (z + 2 * k) % 16), k and q))
     family, cousins = [], []
     for k in (2, 1, 3, 0):
         for o in (1, 0):
@@ -74,7 +79,7 @@
         load.start()
 
     barrier = pltpu.get_barrier_semaphore()
-    others = [d for _, d in evens + plane] + cousins + [sibling]
+    others = [d for _, d in evens + plane] + [d for _, d, far in spots if far] + cousins + [sibling]
     for d in others:
         pl.semaphore_signal(barrier, inc=1, device_id=d, device_id_type=MESH)
 
@@ -369,28 +374,40 @@
     for i, tile in enumerate((direction, direction2, residual)):
         pack(packed.at[i], tile, 0.0)
 
+    for i in range(3):
+        known[group, 2 * i:2 * i + 2, :] = packed[i, level]
+    for _, device in family:
+        push(known.at[group], known.at[group], s_fin.at[0], r_fin.at[0], device)
+
     own = end_plane(2)
     pack(slice_out, own, jnp.broadcast_to(own[9:10], (8, 128)))
-    for slot, device in evens:
-        push(slice_out.at[slot], slice_in.at[level], s_z.at[0], r_z.at[0], device)
-    slice_in[level] = slice_out[level]
+    for slot, device, _ in spots:
+        push(slice_out.at[slot], slice_in.at[x * 8 + level], s_z.at[0], r_z.at[0], device)
+    slice_in[x * 8 + level] = slice_out[level]
     drain()
-    landed(slice_in.at[pl.ds(0, 7)], r_z.at[0])
-    image = total(slice_in, 8)
+    landed(known.at[pl.ds(0, 7)], s_fin.at[0])
+    landed(known.at[pl.ds(0, 7)], r_fin.at[0])
+    landed(slice_in.at[pl.ds(0, 31)], r_z.at[0])
+    for k in range(4):
+        image = slice_in[k * 8]
+        for g in range(1, 8):
+            image = image + slice_in[k * 8 + g]
+        images[c, k] = image
+
+    push(images.at[c], images.at[c], s_img.at[0], r_img.at[0], sibling)
     pick = lax.broadcasted_iota(jnp.int32, (2, 128), 0) * 128 + lax.broadcasted_iota(jnp.int32, (2, 128), 1)
-    product = jnp.sum(jnp.where(pick == 144, image, 0.0), keepdims=True)
+    product = jnp.sum(jnp.where(pick == 144, images[c, 0], 0.0), keepdims=True)
     alpha2 = rz_next / (product + DAMPING * square)
-    fin[group, 0:2, :] = alpha1 * packed[0, level] + alpha2 * packed[1, level]
-    fin[group, 2:4, :] = packed[2, level] - alpha2 * (image + DAMPING * packed[1, level])
-
-    for _, device in family:
-        push(fin.at[group], fin.at[group], s_fin.at[0], r_fin.at[0], device)
-    landed(slice_in.at[pl.ds(0, 7)], s_z.at[0])
-
     scale1 = jnp.concatenate([alpha1] * 4, axis=1)
     scale2 = jnp.concatenate([alpha2] * 4, axis=1)
     lm_o[...] = q_sc[0:3, :] - scale1 * q_sc[3:6, :] - scale2 * q_sc[6:9, :]
-    landed(fin.at[pl.ds(0, 7)], r_fin.at[0])
+    for g in range(8):
+        fin[g, 0:2, :] = alpha1 * known[g, 0:2, :] + alpha2 * known[g, 2:4, :]
+    landed(slice_in.at[pl.ds(0, 31)], s_z.at[0])
+    landed(images.at[0], r_img.at[0])
+    for g in range(8):
+        fin[g, 2:4, :] = known[g, 4:6, :] - alpha2 * (images[g % 2, g // 2] + DAMPING * known[g, 2:4, :])
+
     for i, out in enumerate((step_o, res_o)):
         out[0:8, :] = swap(fin[:, 2 * i, :])
         second = fin[:, 2 * i + 1, :]
@@ -398,7 +415,7 @@
         for g in range(1, 8):
             row = jnp.where(lane[0:1] // 16 == g, pltpu.roll(second, 16 * g, 1)[g:g + 1], row)
         out[8:9, :] = row
-    landed(fin.at[pl.ds(0, 7)], s_fin.at[0])
+    landed(images.at[0], s_img.at[0])
 
 
 def deliver(step, res, lm, step_o, res_o, lm_o):
@@ -421,10 +438,11 @@
         pltpu.VMEM((16, OBS), F32), pltpu.VMEM((8, OBS), F32),
         pltpu.VMEM((3, K, LM), F32), pltpu.VMEM((2, K, LM), F32), pltpu.VMEM((2, K, LM), F32), pltpu.VMEM((8, LM), F32), pltpu.VMEM((16, LM), F32),
         tiles(2, 2, 32), tiles(2, 32), tiles(2, 32), tiles(2, 32, 2), tiles(32, 2), tiles(32, 2), tiles(8, 2), tiles(8),
-        pltpu.VMEM((8, 2, 128), F32), pltpu.VMEM((8, 2, 128), F32), tiles(2, 2, 32), pltpu.VMEM((3, 8, 2, 128), F32),
+        pltpu.VMEM((8, 2, 128), F32), pltpu.VMEM((32, 2, 128), F32), tiles(2, 2, 32), pltpu.VMEM((3, 8, 2, 128), F32),
+        pltpu.VMEM((8, 6, 128), F32), pltpu.VMEM((2, 4, 2, 128), F32),
         pltpu.VMEM((8, 4, 128), F32),
         dma((FLOWS,)), dma((FLOWS,)), dma((FLOWS,)), dma((FLOWS,)), dma((2,)), dma((2,)), dma((1,)), dma((1,)),
-        dma((2,)), dma((2,)), dma((2,)), dma((2,)), dma((1,)), dma((1,)), dma((4,)),
+        dma((2,)), dma((2,)), dma((2,)), dma((2,)), dma((1,)), dma((1,)), dma((1,)), dma((1,)), dma((4,)),
     ]
     out_shape = (jax.ShapeDtypeStruct((9, 128), F32), jax.ShapeDtypeStruct((9, 128), F32), jax.ShapeDtypeStruct((3, LM), F32))
     results = pl.pallas_call(

time: 83 us -> 83.7 us (level)
  no operation moved by 1% of the time
where the time goes in v5:
time: 83.7 us; the launch traced here: 83.5 us
  Pallas kernels  82.8 us (99%)
    pallas_call x1, Pallas kernels, body(): pl.pallas_call(kernel, out_shape=(pltpu.VMEM((9, 128), F32), pltpu.VMEM((...  82.2 us

profile of v5, /device:TPU:1, one launch (start us, length us, event | category | flops | bytes accessed | tf_op | source)
XLA Modules:
  0.0 83.5 jit_solution(6027572827020381744)
XLA Ops:
  0.6 82.2 %schur_cg.1 = (f32[9,128]{1,0:T(8,128)S(1)}, f32[9,128]{1,0:T(8,128)S(1)}, f32[3,512]{1,0:T(4,128)S(1)}) custom-call(f32[2,9,8,512]{3,2,1,0:T(8,128)} %cj_hbm.1, f32[2,3,8,512]{3,2,1,0:T(8,128)} %lj_hbm.1, f32[2,8,512]{2,1,0:T(8,128)} %rs_hbm.1, s32[8,512]{1,0:T(8,128)} %ci_hbm.1), custom_call_target="tpu_custom_call" | custom-call | tf_op jit(solution)/shard_map/schur_cg/pallas_call | solution.py:448
  82.9 0.6 deliver.1
